TPU v7x, 32 devices: a whole 2x2x4 slice. The times are simulated.
32 devices in a mesh: row: 8 (over z, y), col: 4 (over x, core).
Axes of the slice: x: 2, y: 2, z: 4, core: 2. Of those that a mesh axis runs over, the one named last changes fastest.
Arguments:
- features: bfloat16 [8192, 128], P(('col', 'row')), may hold values from -6 to 6
- weight: bfloat16 [128, 256], replicated, may hold values from -0.5 to 0.5
- bias: float32 [256], replicated, may hold values from -3 to 3
- grad_out: bfloat16 [8192, 256], P(('row', 'col')), may hold values from -6 to 6
- tile_values: bfloat16 [8, 4, 128, 128, 128], P('row', 'col'), may hold values from -0.1875 to 0.1875
- tile_rows: int32 [8, 4, 128], P('row', 'col'), may hold values from 0 to 7
- tile_cols: int32 [8, 4, 128], P('row', 'col'), may hold values from 0 to 15
- tile_count: int32 [8, 4], P('row', 'col'), may hold values from 42 to 128, as said below
Outputs:
- hidden: bfloat16 [8192, 256], P(('row', 'col'))
- grad_weight: float32 [128, 256], replicated
- grad_bias: float32 [256], replicated
- grad_features: bfloat16 [8192, 128], P(('col', 'row'))
Inputs may be any that keep to these rules, and one draw needn't show every extreme that they name: `tile_count`: slots below the count are live; some block has all 128 slots live.
All inputs are finite; a program needn't handle non-finite values.
Results may differ from a plain program's by a relative error of at most 0.03.
Values may be sent and summed in bfloat16 or wider, within the bound.
No kernel may reach another device: no remote copies, remote signals or barrier semaphores. Data moves between devices by JAX's collectives and lax.ppermute only.
A program may use at most 64 MiB of HBM per device.

v0:
```python
import jax
import jax.numpy as jnp
from jax import lax
from jax.sharding import PartitionSpec as P


def per_device(features, weight, bias, grad_out, tile_values, tile_rows, tile_cols, tile_count):
    values = tile_values[0, 0]
    slot_rows = tile_rows[0, 0]
    slot_cols = tile_cols[0, 0]
    tile_size = values.shape[1]
    width_in = features.shape[1]
    node_rows = features.shape[0]
    live = (jnp.arange(values.shape[0]) < tile_count[0, 0]).astype(values.dtype)
    values = values * live[:, None, None]
    panel = lax.all_gather(features, "row", axis=0, tiled=True)
    panel_tiles = panel.reshape(-1, tile_size, width_in)
    picked = panel_tiles[slot_cols]
    products = jnp.einsum("kij,kjf->kif", values, picked, preferred_element_type=jnp.float32)
    row_segments = lax.axis_size("col") * node_rows // tile_size
    partial_value = jax.ops.segment_sum(products, slot_rows, num_segments=row_segments).reshape(
        -1, width_in
    )
    aggregate = lax.psum_scatter(
        partial_value.astype(jnp.bfloat16), "col", scatter_dimension=0, tiled=True
    )
    preact = jnp.dot(aggregate, weight, preferred_element_type=jnp.float32) + bias
    sigmoid_pre = jax.nn.sigmoid(preact)
    hidden = (preact * sigmoid_pre).astype(jnp.bfloat16)
    slope_factor = sigmoid_pre * (1.0 + preact * (1.0 - sigmoid_pre))
    grad_pre = (grad_out.astype(jnp.float32) * slope_factor).astype(jnp.bfloat16)
    local_weight = jnp.dot(aggregate.T, grad_pre, preferred_element_type=jnp.float32)
    local_bias = jnp.sum(grad_pre.astype(jnp.float32), axis=0)
    grad_weight, grad_bias = lax.psum((local_weight, local_bias), ("row", "col"))
    grad_block = lax.all_gather(grad_pre, "col", axis=0, tiled=True)
    block_aggregate = jnp.dot(grad_block, weight.T, preferred_element_type=jnp.float32).astype(
        jnp.bfloat16
    )
    block_tiles = block_aggregate.reshape(-1, tile_size, width_in)
    picked_back = block_tiles[slot_rows]
    back_products = jnp.einsum(
        "kji,kjf->kif", values, picked_back, preferred_element_type=jnp.float32
    )
    col_segments = lax.axis_size("row") * node_rows // tile_size
    partial_back = jax.ops.segment_sum(back_products, slot_cols, num_segments=col_segments).reshape(
        -1, width_in
    )
    grad_features = lax.psum_scatter(
        partial_back.astype(jnp.bfloat16), "row", scatter_dimension=0, tiled=True
    )
    return (hidden, grad_weight, grad_bias, grad_features)


def solution(mesh):
    return jax.shard_map(
        per_device,
        mesh=mesh,
        in_specs=(
            P(("col", "row"), None),
            P(),
            P(),
            P(("row", "col"), None),
            P("row", "col", None, None, None),
            P("row", "col", None),
            P("row", "col", None),
            P("row", "col"),
        ),
        out_specs=(P(("row", "col"), None), P(), P(), P(("col", "row"), None)),
        check_vma=False,
    )
```

profile of v0, /device:TPU:0, one launch (start us, length us, event | category | flops | bytes accessed | tf_op | source)
XLA Modules:
  0.0 299.1 jit_solution(12727393538970302831)
XLA Ops:
  7.2 0.0 copy-start
  7.2 0.0 reduce-scatter.3.cloned.1.call-start
  7.9 33.2 %all_gather.6 = bf16[2048,128]{1,0:T(8,128)(2,1)S(1)} all-gather(bf16[256,128]{1,0:T(8,128)(2,1)} %param.8), channel_id=1, replica_groups=mesh['row'=8,'col'=4] {'row'}, dimensions={0}, use_global_device_ids=true | all-gather | bytes 589824 | tf_op jit(solution)/shard_map/all_gather | solution.py:16
  41.1 0.7 fusion.4
  41.8 3.1 %gather_fusion = bf16[128,128,128]{2,1,0:T(8,128)(2,1)} fusion(bf16[16,128,128]{2,1,0:T(8,128)(2,1)S(1)} %bitcast.29, s32[1024]{0:T(1024)S(1)} %pad_clamp_fusion.1), kind=kCustom, calls=%fused_computation | custom fusion | bytes 8389120 | tf_op jit(solution)/shard_map/gather | solution.py:18
  44.8 0.0 copy-start.1
  44.8 8.0 %fusion.1 = f32[128,128,128]{2,1,0:T(8,128)} fusion(bf16[128,128,128]{2,1,0:T(8,128)(2,1)} %gather_fusion, bf16[1,1,128,128,128]{4,3,2,1,0:T(8,128)(2,1)} %param.12, bf16[128]{0:T(256)(128)(2,1)S(1)} %compare_convert_fusion), kind=kOutput, calls=%fused_computation.6 | convolution fusion | flops 538968064 | bytes 16777472 | tf_op jit(solution)/shard_map/kij,kjf->kif/dot_general | solution.py:19
  52.9 0.0 copy-done.1
  52.9 0.0 copy-start.3
  52.9 0.0 copy-start.4
  52.9 17.0 %scatter_fusion = f32[8,128,128]{2,1,0:T(8,128)S(1)} fusion(f32[8,128,128]{2,1,0:T(8,128)S(1)} %broadcast_in_dim.4, s32[128]{0:T(128)S(1)} %bitcast.32, f32[128,128,128]{2,1,0:T(8,128)} %fusion.1), kind=kCustom, calls=%fused_computation.2 | custom fusion | flops 2097152 | bytes 25166336 | tf_op jit(solution)/shard_map/scatter-add | solution.py:21
  69.9 0.7 convert_element_type.35
  70.7 0.0 reduce-scatter.3.cloned.1.call-update
  70.7 0.0 all-reduce.2.cloned.1.call-start
  70.8 21.2 %reduce-scatter.3.cloned.1.call-done = bf16[256,128]{1,0:T(8,128)(2,1)} async-done(((bf16[1024,128]{1,0:T(8,128)(2,1)}), bf16[256,128]{1,0:T(8,128)(2,1)}) %reduce-scatter.3.cloned.1.call-update) | async-done | bytes 65552 | tf_op jit(solution)/shard_map/reduce_scatter | solution.py:24
  92.0 0.0 copy-done
  92.0 0.0 copy-done.3
  92.0 0.0 copy-done.4
  92.0 1.8 convert_reduce_fusion
  93.8 6.7 %all_gather.7 = bf16[1024,256]{1,0:T(8,128)(2,1)S(1)} all-gather(bf16[256,256]{1,0:T(8,128)(2,1)S(1)} %get-tuple-element.5), channel_id=1, replica_groups=mesh['row'=8,'col'=4] {'col'}, dimensions={0}, use_global_device_ids=true | all-gather | bytes 655360 | tf_op jit(solution)/shard_map/all_gather | solution.py:35
  100.5 1.7 fusion.6
  102.2 0.0 all-reduce.2.cloned.1.call-update
  102.2 0.0 reduce-scatter.5.cloned.1.call-start
  102.3 0.3 convolution_convert_fusion
  102.6 3.1 %gather_fusion.1 = bf16[128,128,128]{2,1,0:T(8,128)(2,1)} fusion(bf16[8,128,128]{2,1,0:T(8,128)(2,1)S(1)} %bitcast.28, s32[1024]{0:T(1024)S(1)} %pad_clamp_fusion), kind=kCustom, calls=%fused_computation.1 | custom fusion | bytes 8389120 | tf_op jit(solution)/shard_map/gather | solution.py:40
  105.6 0.0 copy-start.2
  105.6 8.4 %fusion = f32[128,128,128]{2,1,0:T(8,128)} fusion(bf16[128,128,128]{2,1,0:T(8,128)(2,1)} %gather_fusion.1, bf16[1,1,128,128,128]{4,3,2,1,0:T(8,128)(2,1)} %param.12, bf16[128]{0:T(256)(128)(2,1)S(1)} %compare_convert_fusion), kind=kOutput, calls=%fused_computation.5 | convolution fusion | flops 538968064 | bytes 16777472 | tf_op jit(solution)/shard_map/kji,kjf->kif/dot_general | solution.py:41
  114.0 0.1 broadcast_in_dim.5
  114.1 0.0 copy-done.2
  114.1 17.1 %scatter_fusion.1 = f32[16,128,128]{2,1,0:T(8,128)S(1)} fusion(f32[16,128,128]{2,1,0:T(8,128)S(1)} %broadcast_in_dim.5, s32[128]{0:T(128)S(1)} %bitcast.33, f32[128,128,128]{2,1,0:T(8,128)} %fusion), kind=kCustom, calls=%fused_computation.3 | custom fusion | flops 2097152 | bytes 25166336 | tf_op jit(solution)/shard_map/scatter-add | solution.py:45
  131.2 0.9 convert_element_type.42
  132.1 0.0 reduce-scatter.5.cloned.1.call-update
  132.1 39.8 %psum.15 = f32[256]{0:T(256)} all-reduce(f32[256]{0:T(256)S(1)} %get-tuple-element.4), channel_id=1, replica_groups=mesh['row'=8,'col'=4] {'row','col'}, use_global_device_ids=true, to_apply=%region_4.0 | all-reduce | flops 256 | bytes 2048 | tf_op jit(solution)/shard_map/psum | solution.py:34
  171.9 53.3 %all-reduce.2.cloned.1.call-done = f32[128,256]{1,0:T(8,128)} async-done(((f32[128,256]{1,0:T(8,128)}), f32[128,256]{1,0:T(8,128)}) %all-reduce.2.cloned.1.call-update) | async-done | bytes 131088 | tf_op jit(solution)/shard_map/psum | solution.py:34
  225.2 65.7 %reduce-scatter.5.cloned.1.call-done = bf16[256,128]{1,0:T(8,128)(2,1)} async-done(((bf16[2048,128]{1,0:T(8,128)(2,1)}), bf16[256,128]{1,0:T(8,128)(2,1)}) %reduce-scatter.5.cloned.1.call-update) | async-done | bytes 65552 | tf_op jit(solution)/shard_map/reduce_scatter | solution.py:48
  291.0 1.6 copy.18
  (5 shorter events, 0.1 us)
Async XLA Ops:
  7.2 84.8 %copy-start = (bf16[128,256]{1,0:T(8,128)(2,1)S(1)}, bf16[128,256]{1,0:T(8,128)(2,1)}, u32[]{:S(2)}) copy-start(bf16[128,256]{1,0:T(8,128)(2,1)} %param.9) | copy-start | bytes 196612
  7.2 84.8 %reduce-scatter.3.cloned.1.call-start = ((), (), s32[]{:S(2)}) async-start(), calls=%async_computation.2 | async-start | bytes 327680 | tf_op jit(solution)/shard_map/reduce_scatter | solution.py:24
  44.8 8.0 %copy-start.1 = (s32[1,1,128]{2,1,0:T(1,128)S(1)}, s32[1,1,128]{2,1,0:T(1,128)}, u32[]{:S(2)}) copy-start(s32[1,1,128]{2,1,0:T(1,128)} %param.13) | copy-start | bytes 1540
  52.9 39.1 %copy-start.3 = (bf16[256,256]{1,0:T(8,128)(2,1)S(1)}, bf16[256,256]{1,0:T(8,128)(2,1)}, u32[]{:S(2)}) copy-start(bf16[256,256]{1,0:T(8,128)(2,1)} %param.11) | copy-start | bytes 393220
  52.9 39.1 %copy-start.4 = (f32[256]{0:T(256)S(1)}, f32[256]{0:T(256)}, u32[]{:S(2)}) copy-start(f32[256]{0:T(256)} %param.10) | copy-start | bytes 3076
  70.7 154.5 %all-reduce.2.cloned.1.call-start = ((), (), s32[]{:S(2)}) async-start(), calls=%async_computation.3 | async-start | bytes 262144 | tf_op jit(solution)/shard_map/psum | solution.py:34
  102.2 188.8 %reduce-scatter.5.cloned.1.call-start = ((), (), s32[]{:S(2)}) async-start(), calls=%async_computation.4 | async-start | bytes 589824 | tf_op jit(solution)/shard_map/reduce_scatter | solution.py:48
  105.6 8.5 %copy-start.2 = (s32[1,1,128]{2,1,0:T(1,128)S(1)}, s32[1,1,128]{2,1,0:T(1,128)}, u32[]{:S(2)}) copy-start(s32[1,1,128]{2,1,0:T(1,128)} %param.14) | copy-start | bytes 1540
Sparse Core Ops, SparseCore 0:
  70.8 21.1 reduce-scatter.2
  102.3 122.8 all-reduce.1
  229.5 61.3 reduce-scatter.4
where the time goes:
time: 300 us; the launch traced here: 299 us
  waiting for transfers between devices  140 us (47%)
  blocking collectives  79.7 us (27%)
  other arithmetic  36.4 us (12%)
  matrix products  20.2 us (7%)
  between operations  14.5 us (5%)
  local copies, waits for them, and re-layouts  7.84 us (3%)
    reduce_scatter x1, waiting for transfers between devices, per_device(): lax.psum_scatter(partial_back.astype(jnp.bfloat16), 'row', scatter_dimens...  65.7 us
    psum x1, waiting for transfers between devices, per_device(): lax.psum((local_weight, local_bias), ('row', 'col'))  53.3 us
    psum x1, blocking collectives, per_device(): lax.psum((local_weight, local_bias), ('row', 'col'))  39.8 us
    all_gather x1, blocking collectives, per_device(): panel = lax.all_gather(features, 'row', axis=0, tiled=True)  33.2 us
    reduce_scatter x1, waiting for transfers between devices, per_device(): lax.psum_scatter(partial_value.astype(jnp.bfloat16), 'col', scatter_dimen...  21.2 us
    scatter-add x1, other arithmetic, per_device(): jax.ops.segment_sum(back_products, slot_cols, num_segments=col_segments)  17.1 us
    scatter-add x1, other arithmetic, per_device(): jax.ops.segment_sum(products, slot_rows, num_segments=row_segments)  17 us
    dot_general x1, matrix products, per_device(): jnp.einsum('kji,kjf->kif', values, picked_back, preferred_element_type=jn...  8.4 us
  transfers between devices with their start and end apart: 3, of which 3 were waited for; matrix products, arithmetic and copies ran while one was open for 10% of the time, Pallas kernels for 0%

commit v1 on v0

v1 whole, which is shorter than its diff:
```python
import functools

import jax
import jax.numpy as jnp
from jax import lax
from jax.experimental import pallas as pl
from jax.experimental.pallas import tpu as pltpu
from jax.sharding import PartitionSpec as P

BF16 = jnp.bfloat16
F32 = jnp.float32
VMEM_LIMIT = 32 * 1024 * 1024
IN_VMEM = pl.BlockSpec(memory_space=pltpu.VMEM)
IN_ANY = pl.BlockSpec(memory_space=pl.ANY)
FIRST = 1 << 35
SOON = 3 << 28


def call(kernel, out_shape, in_specs, scratch=(), flops=0, nbytes=0, after=()):
    multi = isinstance(out_shape, (list, tuple))
    first, last = len(in_specs), len(in_specs) + len(after)

    def body(*refs):
        kernel(*refs[:first], *refs[last:])

    run = pl.pallas_call(
        body,
        out_shape=out_shape,
        in_specs=list(in_specs) + [IN_ANY] * len(after),
        out_specs=[IN_VMEM] * len(out_shape) if multi else IN_VMEM,
        scratch_shapes=list(scratch),
        compiler_params=pltpu.CompilerParams(vmem_limit_bytes=VMEM_LIMIT),
        cost_estimate=pl.CostEstimate(flops=flops, bytes_accessed=nbytes, transcendentals=0),
    )
    return lambda *args: run(*args, *after)


def lists_kernel(places, lists):
    slots, wide = places.shape[1], lists.shape[1]
    by_slot = jnp.broadcast_to(places[...].astype(F32), (slots, slots))
    down = by_slot.T[:, :1]
    slot = lax.broadcasted_iota(jnp.int32, (slots, wide), 0)
    at = lax.broadcasted_iota(jnp.int32, (slots, wide), 1)
    none = jnp.float32(slots)
    first = jnp.where(down == at.astype(F32), slot.astype(F32), none)
    lists[0:1, :] = jnp.min(first, axis=0, keepdims=True).astype(jnp.int32)
    later = slot[:, :slots] > at[:, :slots]
    follow = jnp.where((down == by_slot) & later, slot[:, :slots].astype(F32), none)
    lists[1:2, :slots] = jnp.min(follow, axis=0, keepdims=True).astype(jnp.int32)
    lists[1:2, slots:] = jnp.full((1, wide - slots), slots, jnp.int32)


def densify_kernel(lists, values, dense, head, after, many, list_sems):
    slots, tile, _ = values.shape
    row_tiles, col_tiles = dense.shape[0] // tile, dense.shape[1] // tile
    moves = [
        pltpu.make_async_copy(lists.at[pl.ds(0, 1)], head, list_sems.at[0]),
        pltpu.make_async_copy(lists.at[pl.ds(1, 1)], after, list_sems.at[1]),
    ]
    for copy in moves:
        copy.start()
    for copy in moves:
        copy.wait()

    def held(slot):
        return jnp.where(slot < slots, values[jnp.minimum(slot, slots - 1)], 0)

    def write(row, found):
        top = pl.ds(pl.multiple_of(row * tile, tile), tile)
        for col in range(col_tiles):
            place = row * col_tiles + col
            one = head[0, place]
            two = after[0, one]
            dense[top, col * tile : (col + 1) * tile] = held(one) + held(two)
            many[found] = place
            found += (after[0, two] < slots).astype(jnp.int32)
        return found

    found = lax.fori_loop(0, row_tiles, write, jnp.int32(0))

    def rewrite(at, carry):
        place = many[at]
        row = place // col_tiles
        top = pl.ds(pl.multiple_of(row * tile, tile), tile)
        left = pl.ds(pl.multiple_of((place - row * col_tiles) * tile, tile), tile)

        def more(state):
            slot, total = state
            return after[0, slot], total + values[slot].astype(F32)

        _, total = lax.while_loop(
            lambda state: state[0] < slots, more, (head[0, place], jnp.zeros((tile, tile), F32))
        )
        dense[top, left] = total.astype(BF16)
        return carry

    lax.fori_loop(0, found, rewrite, 0)


def forward_kernel(dense, own, y_1, near, y_near, far_4, y_4, far_6, out):
    pieces = (own, y_1, near, y_near, far_4, y_4, far_6)
    nodes = own.shape[0]
    r, c = lax.axis_index("row"), lax.axis_index("col")
    for at, j in enumerate((1, 3, 0, 2)):
        top = pl.ds(pl.multiple_of((c ^ j) * nodes, nodes), nodes)
        acc = jnp.zeros(own.shape, F32)
        for i, piece in enumerate(pieces):
            left = pl.ds(pl.multiple_of((r ^ i) * nodes, nodes), nodes)
            acc += jnp.dot(dense[top, left], piece[...], preferred_element_type=F32)
        out[at * nodes : (at + 1) * nodes, :] = acc


def finish_kernel(start, dense, most, y_6, out):
    nodes = y_6.shape[0]
    r, c = lax.axis_index("row"), lax.axis_index("col")
    left = pl.ds(pl.multiple_of((r ^ 7) * nodes, nodes), nodes)
    for at in range(2):
        j = (1, 3, 0, 2)[start + at]
        top = pl.ds(pl.multiple_of((c ^ j) * nodes, nodes), nodes)
        acc = most[(start + at) * nodes : (start + at + 1) * nodes, :]
        acc += jnp.dot(dense[top, left], y_6[...], preferred_element_type=F32)
        out[at * nodes : (at + 1) * nodes, :] = acc.astype(out.dtype)


def add_kernel(own, other, out):
    out[...] = (own[...] + other[...].astype(F32)).astype(out.dtype)


def layer_kernel(own, other, weight, bias, grad_out, grad_out_x, aggregate_out, grad_pre_out, hidden, grad_aggregate):
    nodes = hidden.shape[0]
    for at, grads in enumerate((grad_out, grad_out_x)):
        here = slice(at * nodes, (at + 1) * nodes)
        there = slice((1 - at) * nodes, (2 - at) * nodes)
        aggregate = (own[here, :].astype(F32) + other[there, :].astype(F32)).astype(BF16)
        aggregate_out[here, :] = aggregate
        preact = jnp.dot(aggregate, weight[...], preferred_element_type=F32) + bias[...]
        sig = jax.nn.sigmoid(preact)
        if at == 0:
            hidden[...] = (preact * sig).astype(BF16)
        slope = sig * (1.0 + preact * (1.0 - sig))
        grad_pre = (grads[...].astype(F32) * slope).astype(BF16)
        grad_pre_out[here, :] = grad_pre
        grad_aggregate[here, :] = lax.dot_general(
            grad_pre, weight[...], (((1,), (1,)), ((), ())), preferred_element_type=F32
        ).astype(BF16)


def pack(out, weights, bias):
    rows = weights.shape[0]
    high = bias.astype(BF16)
    low = (bias - high.astype(F32)).astype(BF16)
    at = lax.broadcasted_iota(jnp.int32, (out.shape[0] - rows, out.shape[1]), 0)
    out[:rows, :] = weights.astype(BF16)
    out[rows:, :] = jnp.where(at == 0, high.astype(F32), jnp.where(at == 1, low.astype(F32), 0.0)).astype(BF16)


def unpack(ref, rows):
    last = ref[rows:, :].astype(F32)
    return ref[:rows, :].astype(F32), last[0:1, :] + last[1:2, :]


def weight_kernel(aggregate, grad_pre, mine, theirs, full):
    core = lax.axis_index("col") & 1
    nodes = aggregate.shape[0] // 2
    first, second = slice(0, nodes), slice(nodes, 2 * nodes)
    by_node = (((0,), (0,)), ((), ()))
    full[...] = lax.dot_general(
        aggregate[first, :], grad_pre[first, :], by_node, preferred_element_type=F32
    ) + lax.dot_general(aggregate[second, :], grad_pre[second, :], by_node, preferred_element_type=F32)
    bias = jnp.sum(grad_pre[first, :].astype(F32), axis=0, keepdims=True) + jnp.sum(
        grad_pre[second, :].astype(F32), axis=0, keepdims=True
    )
    rows = full.shape[0] // 2
    for out, half in ((mine, core), (theirs, 1 - core)):
        pack(out, full[pl.ds(pl.multiple_of(half * rows, rows), rows), :], bias)


def merge_kernel(rows, own, other, out):
    weights, bias = unpack(own, rows)
    more_weights, more_bias = unpack(other, rows)
    pack(out, weights + more_weights, bias + more_bias)


def last_merge_kernel(own, near, half, bias):
    rows = half.shape[0]
    weights, biases = unpack(own, rows)
    more_weights, more_biases = unpack(near.at[near.shape[0] - own.shape[0] :], rows)
    half[...] = weights + more_weights
    bias[...] = biases + more_biases


def kept_kernel(places, dense, own, other, hidden_in, out, hidden):
    hidden[...] = hidden_in[...]
    backward_kernel(places, dense, own, other, out)


def backward_kernel(places, dense, own, other, out):
    nodes = own.shape[0] // 2
    r, c = lax.axis_index("row"), lax.axis_index("col")
    turned = [
        (j, ref[at * nodes : (at + 1) * nodes, :].T)
        for j, ref, at in ((0, own, 0), (2, own, 1), (1, other, 0), (3, other, 1))
    ]
    for at, i in enumerate(places):
        left = pl.ds(pl.multiple_of((r ^ i) * nodes, nodes), nodes)
        acc = jnp.zeros(out.shape[1:], F32)
        for j, piece in turned:
            top = pl.ds(pl.multiple_of((c ^ j) * nodes, nodes), nodes)
            acc += jnp.dot(piece, dense[top, left], preferred_element_type=F32)
        out[at] = acc.astype(out.dtype)


def far_kernel(kept, arrived, first, second):
    first[...] = (kept[0] + arrived[0].astype(F32)).astype(BF16)
    second[...] = (kept[1] + arrived[1].astype(F32)).astype(BF16)


def near_kernel(kept, arrived, part, near):
    rows = kept.shape[1]
    near[:rows, :] = (kept[3] + arrived[1].astype(F32)).astype(BF16)
    near[rows:, :] = part[...]


def gather_far_kernel(share_4, share_6, total):
    total[...] = share_4[...].astype(F32) + share_6[...].astype(F32)


def gather_near_kernel(arrived, near, gathered, total):
    total[...] = arrived[0].astype(F32) + near[: total.shape[0], :].astype(F32) + gathered[...]


def gather_own_kernel(kept, gathered, total):
    total[...] = kept[2] + gathered[...]


def last_kernel(gathered, mine, theirs, bias, grad_features, grad_weight, grad_bias):
    grad_features[...] = gathered[...].T.astype(BF16)
    grad_bias[...] = bias[...]
    core = lax.axis_index("col") & 1
    rows = mine.shape[0]
    for piece, half in ((mine, core), (theirs, 1 - core)):
        grad_weight[pl.ds(pl.multiple_of(half * rows, rows), rows), :] = piece[...]


def swap(value, axis, bits):
    size = lax.axis_size(axis)
    return lax.ppermute(value, axis, [(at, at ^ bits) for at in range(size)])


def dense_block(features, weight, bias, grad_out, tile_values, tile_rows, tile_cols, tile_count):
    n_row, n_col = lax.axis_size("row"), lax.axis_size("col")
    slots, tile = tile_values.shape[2:4]
    nodes, width_in = features.shape
    width_out = weight.shape[1]
    height, length = n_col * nodes, n_row * nodes
    positions = (height // tile) * (length // tile)
    whole = 2 * height * length * width_in
    shape = jax.ShapeDtypeStruct

    far = [swap(features, "row", 4), swap(features, "row", 6)]
    near = swap(features, "row", 2)
    grad_out_x = swap(grad_out, "col", 2)
    y_1, y_near = swap(features, "row", 1), swap(near, "row", 1)
    y_4, y_6 = swap(far[0], "row", 1), swap(far[1], "row", 1)
    places = jnp.where(
        jnp.arange(slots, dtype=jnp.int32) < tile_count[0, 0],
        tile_rows[0, 0] * (length // tile) + tile_cols[0, 0],
        positions,
    ).reshape(1, slots)
    wide = 128 * pl.cdiv(max(positions, slots + 1), 128)
    lists = call(lists_kernel, shape((2, wide), jnp.int32), [IN_VMEM], flops=FIRST)(places)
    dense = call(
        densify_kernel,
        shape((height, length), BF16),
        [IN_VMEM] * 2,
        [
            pltpu.SMEM((1, wide), jnp.int32),
            pltpu.SMEM((1, wide), jnp.int32),
            pltpu.SMEM((positions + 1,), jnp.int32),
            pltpu.SemaphoreType.DMA((2,)),
        ],
        nbytes=2 * tile_values.size * 2,
    )(lists, tile_values.reshape(slots, tile, tile))
    most = call(
        forward_kernel,
        shape((4 * nodes, width_in), F32),
        [IN_VMEM] * 8,
        flops=FIRST,
        nbytes=2 * height * length,
    )(dense, features, y_1, near, y_near, far[0], y_4, far[1])

    def finish(start, dtype):
        return call(
            functools.partial(finish_kernel, start),
            shape((2 * nodes, width_in), dtype),
            [IN_VMEM] * 3,
            flops=whole // 16,
            nbytes=height * length // 8,
        )(dense, most, y_6)

    core_share = swap(finish(0, BF16), "col", 1)
    half = call(
        add_kernel,
        shape((2 * nodes, width_in), BF16),
        [IN_VMEM] * 2,
        nbytes=16 * nodes * width_in,
        after=[grad_out_x],
    )(finish(2, F32), core_share)
    half_x = swap(half, "col", 2)
    aggregate, grad_pre, hidden, grad_aggregate = call(
        layer_kernel,
        [
            shape((2 * nodes, width_in), BF16),
            shape((2 * nodes, width_out), BF16),
            shape((nodes, width_out), BF16),
            shape((2 * nodes, width_in), BF16),
        ],
        [IN_VMEM] * 6,
        flops=8 * nodes * width_in * width_out,
        nbytes=16 * nodes * width_out,
    )(half, half_x, weight, bias.reshape(1, -1), grad_out, grad_out_x)
    grad_aggregate_core = swap(grad_aggregate, "col", 1)

    def backward(parts, dtype, after=()):
        return call(
            functools.partial(backward_kernel, parts),
            shape((len(parts), width_in, nodes), dtype),
            [IN_VMEM] * 3,
            flops=whole * len(parts) // n_row,
            nbytes=height * length * 2 * len(parts) // n_row,
            after=after,
        )(dense, grad_aggregate, grad_aggregate_core)

    sent_far = backward((5, 7), BF16)
    arrived_far = swap(sent_far, "row", 1)
    kept, hidden = call(
        functools.partial(kept_kernel, (4, 6, 0, 1)),
        [shape((4, width_in, nodes), F32), shape(hidden.shape, BF16)],
        [IN_VMEM] * 4,
        flops=whole // 2,
        nbytes=height * length,
        after=[sent_far],
    )(dense, grad_aggregate, grad_aggregate_core, hidden)
    turned = shape((width_in, nodes), BF16)
    share_4, share_6 = call(far_kernel, [turned] * 2, [IN_VMEM] * 2, nbytes=16 * nodes * width_in)(
        kept, arrived_far
    )

    mine, theirs = call(
        weight_kernel,
        [shape((width_in // 2 + 16, width_out), BF16)] * 2,
        [IN_VMEM] * 2,
        [pltpu.VMEM((width_in, width_out), F32)],
        flops=4 * nodes * width_in * width_out,
        nbytes=8 * width_in * width_out,
    )(aggregate, grad_pre)

    def merge(own, other, after=()):
        return call(
            functools.partial(merge_kernel, width_in // 2),
            shape(own.shape, BF16),
            [IN_VMEM] * 2,
            nbytes=6 * own.size,
            after=after,
        )(own, other)

    part = merge(mine, swap(theirs, "col", 1), [sent_far])
    part = merge(part, swap(part, "row", 2))
    sent_near = backward((2, 3), BF16, [part])
    arrived_near = swap(sent_near, "row", 2)
    part = merge(part, swap(part, "row", 4))
    near = call(
        near_kernel,
        shape((width_in + part.shape[0], nodes), BF16),
        [IN_VMEM] * 3,
        nbytes=8 * nodes * width_in,
    )(kept, arrived_near, part)
    near = swap(near, "row", 1)
    half_weight, bias_sum = call(
        last_merge_kernel,
        [shape((width_in // 2, width_out), F32), shape((1, width_out), F32)],
        [IN_VMEM] * 2,
        nbytes=8 * part.size,
    )(part, near)
    turned = shape((width_in, nodes), F32)
    gathered = call(gather_far_kernel, turned, [IN_VMEM] * 2, flops=SOON)(
        swap(share_4, "row", 4), swap(share_6, "row", 6)
    )
    gathered = call(gather_near_kernel, turned, [IN_VMEM] * 3)(arrived_near, near, gathered)
    gathered = call(gather_own_kernel, turned, [IN_VMEM] * 2, flops=FIRST)(kept, gathered)
    grad_features, grad_weight, grad_bias = call(
        last_kernel,
        [
            shape((nodes, width_in), BF16),
            shape((width_in, width_out), F32),
            shape((1, width_out), F32),
        ],
        [IN_VMEM] * 4,
        nbytes=16 * nodes * width_in,
    )(gathered, half_weight, swap(half_weight, "col", 1), bias_sum)
    return hidden, grad_weight, grad_bias.reshape(-1), grad_features


def sparse_block(features, weight, bias, grad_out, tile_values, tile_rows, tile_cols, tile_count):
    values = tile_values[0, 0]
    slot_rows = tile_rows[0, 0]
    slot_cols = tile_cols[0, 0]
    tile_size = values.shape[1]
    width_in = features.shape[1]
    node_rows = features.shape[0]
    live = (jnp.arange(values.shape[0]) < tile_count[0, 0]).astype(values.dtype)
    values = values * live[:, None, None]
    panel = lax.all_gather(features, "row", axis=0, tiled=True)
    panel_tiles = panel.reshape(-1, tile_size, width_in)
    picked = panel_tiles[slot_cols]
    products = jnp.einsum("kij,kjf->kif", values, picked, preferred_element_type=F32)
    row_segments = lax.axis_size("col") * node_rows // tile_size
    partial_value = jax.ops.segment_sum(products, slot_rows, num_segments=row_segments).reshape(
        -1, width_in
    )
    aggregate = lax.psum_scatter(
        partial_value.astype(BF16), "col", scatter_dimension=0, tiled=True
    )
    preact = jnp.dot(aggregate, weight, preferred_element_type=F32) + bias
    sigmoid_pre = jax.nn.sigmoid(preact)
    hidden = (preact * sigmoid_pre).astype(BF16)
    slope_factor = sigmoid_pre * (1.0 + preact * (1.0 - sigmoid_pre))
    grad_pre = (grad_out.astype(F32) * slope_factor).astype(BF16)
    local_weight = jnp.dot(aggregate.T, grad_pre, preferred_element_type=F32)
    local_bias = jnp.sum(grad_pre.astype(F32), axis=0)
    grad_weight, grad_bias = lax.psum((local_weight, local_bias), ("row", "col"))
    grad_aggregate = jnp.dot(grad_pre, weight.T, preferred_element_type=F32).astype(BF16)
    block_aggregate = lax.all_gather(grad_aggregate, "col", axis=0, tiled=True)
    block_tiles = block_aggregate.reshape(-1, tile_size, width_in)
    picked_back = block_tiles[slot_rows]
    back_products = jnp.einsum(
        "kji,kjf->kif", values, picked_back, preferred_element_type=F32
    )
    col_segments = lax.axis_size("row") * node_rows // tile_size
    partial_back = jax.ops.segment_sum(back_products, slot_cols, num_segments=col_segments).reshape(
        -1, width_in
    )
    grad_features = lax.psum_scatter(
        partial_back.astype(BF16), "row", scatter_dimension=0, tiled=True
    )
    return hidden, grad_weight, grad_bias, grad_features


def per_device(features, weight, bias, grad_out, tile_values, tile_rows, tile_cols, tile_count):
    n_row, n_col = lax.axis_size("row"), lax.axis_size("col")
    slots, tile = tile_values.shape[2:4]
    nodes = features.shape[0]
    positions = n_row * n_col * (nodes // tile) ** 2
    block = dense_block if (n_row, n_col) == (8, 4) and positions <= 2 * slots else sparse_block
    return block(features, weight, bias, grad_out, tile_values, tile_rows, tile_cols, tile_count)


def solution(mesh):
    return jax.shard_map(
        per_device,
        mesh=mesh,
        in_specs=(
            P(("col", "row"), None),
            P(),
            P(),
            P(("row", "col"), None),
            P("row", "col", None, None, None),
            P("row", "col", None),
            P("row", "col", None),
            P("row", "col"),
        ),
        out_specs=(P(("row", "col"), None), P(), P(), P(("col", "row"), None)),
        check_vma=False,
    )
```

time: 300 us -> 48.9 us (0.16)
  waiting for transfers between devices: 140 us -> 17.8 us
  blocking collectives: 79.7 us -> 0 us
  other arithmetic: 36.4 us -> 0.68 us
  starting transfers between devices: 0.12 us -> 20.9 us
  matrix products: 20.2 us -> 0 us
  between operations: 14.5 us -> 1.51 us
  local copies, waits for them, and re-layouts: 7.84 us -> 0.03 us
  Pallas kernels: 0 us -> 7.76 us
    reduce_scatter x2 -> x0, waiting for transfers between devices: 87 us -> none  [the longest x1 65.7 us: per_device(): lax.psum_scatter(partial_back.astype(jnp.bfloat16), 'row', scatter_dimens...]
    psum x1 -> x0, waiting for transfers between devices: 53.3 us -> none  [per_device(): lax.psum((local_weight, local_bias), ('row', 'col'))]
    all_gather x2 -> x0, blocking collectives: 39.9 us -> none  [the longest x1 33.2 us: per_device(): panel = lax.all_gather(features, 'row', axis=0, tiled=True)]
    psum x1 -> x0, blocking collectives: 39.8 us -> none  [per_device(): lax.psum((local_weight, local_bias), ('row', 'col'))]
    scatter-add x2 -> x0, other arithmetic: 34.1 us -> none  [the longest x1 17.1 us: per_device(): jax.ops.segment_sum(back_products, slot_cols, num_segments=col_segments)]
    ppermute x0 -> x20, starting transfers between devices: none -> 20.9 us  [swap(): return lax.ppermute(value, axis, [(at, at ^ bits) for at in range(size)])]
    dot_general x5 -> x0, matrix products: 20.2 us -> none  [the longest x1 8.4 us: per_device(): jnp.einsum('kji,kjf->kif', values, picked_back, preferred_element_type=jn...]
    ppermute x0 -> x20, waiting for transfers between devices: none -> 17.8 us  [swap(): return lax.ppermute(value, axis, [(at, at ^ bits) for at in range(size)])]
  transfers between devices with their start and end apart: 3 -> 20, of which waited for: 3 -> 8; matrix products, arithmetic and copies ran while one was open for 10% -> 1% of each run, Pallas kernels for 0% -> 13%
where the time goes in v1:
time: 48.9 us; the launch traced here: 48.6 us
  starting transfers between devices  20.9 us (43%)
  waiting for transfers between devices  17.8 us (36%)
  Pallas kernels  7.76 us (16%)
  between operations  1.51 us (3%)
  other arithmetic  0.68 us (1%)
    ppermute x20, starting transfers between devices, swap(): return lax.ppermute(value, axis, [(at, at ^ bits) for at in range(size)])  20.9 us
    ppermute x20, waiting for transfers between devices, swap(): return lax.ppermute(value, axis, [(at, at ^ bits) for at in range(size)])  17.8 us
    pallas_call x21, Pallas kernels, call(): return lambda *args: run(*args, *after)  7.76 us
  transfers between devices with their start and end apart: 20, of which 8 were waited for; matrix products, arithmetic and copies ran while one was open for 1% of the time, Pallas kernels for 13%

profile of v1, /device:TPU:0, one launch (start us, length us, event | category | flops | bytes accessed | tf_op | source)
XLA Modules:
  0.0 48.6 jit_solution(17960446370547892798)
XLA Ops:
  0.6 4.1 %collective-permute-start.3 = (bf16[256,128]{1,0:T(8,128)(2,1)}, bf16[256,128]{1,0:T(8,128)(2,1)S(1)}, u32[]{:S(2)}, u32[]{:S(2)}) collective-permute-start(bf16[256,128]{1,0:T(8,128)(2,1)} %refs_1_.1), channel_id=1, source_target_pairs={{0,16},{4,20},{8,24},{12,28},{16,0},{20,4},{24,8},{28,12},{1,17},{... | collective-permute-start | bytes 196616 | tf_op jit(solution)/shard_map/ppermute | solution.py:247
  4.7 1.6 %collective-permute-start.1 = (bf16[256,128]{1,0:T(8,128)(2,1)}, bf16[256,128]{1,0:T(8,128)(2,1)S(1)}, u32[]{:S(2)}, u32[]{:S(2)}) collective-permute-start(bf16[256,128]{1,0:T(8,128)(2,1)} %refs_1_.1), channel_id=1, source_target_pairs={{0,8},{4,12},{8,0},{12,4},{16,24},{20,28},{24,16},{28,20},{1,9},{5... | collective-permute-start | bytes 196616 | tf_op jit(solution)/shard_map/ppermute | solution.py:247
  6.3 1.5 %collective-permute-start = (bf16[256,128]{1,0:T(8,128)(2,1)}, bf16[256,128]{1,0:T(8,128)(2,1)S(1)}, u32[]{:S(2)}, u32[]{:S(2)}) collective-permute-start(bf16[256,128]{1,0:T(8,128)(2,1)} %refs_1_.1), channel_id=1, source_target_pairs={{0,4},{4,0},{8,12},{12,8},{16,20},{20,16},{24,28},{28,24},{1,5},{5... | collective-permute-start | bytes 196616 | tf_op jit(solution)/shard_map/ppermute | solution.py:247
  7.8 0.2 collective-permute-start.5
  8.1 1.5 %collective-permute-start.8 = (bf16[256,256]{1,0:T(8,128)(2,1)}, bf16[256,256]{1,0:T(8,128)(2,1)S(1)}, u32[]{:S(2)}, u32[]{:S(2)}) collective-permute-start(bf16[256,256]{1,0:T(8,128)(2,1)} %refs_4_.1), channel_id=1, source_target_pairs={{0,2},{1,3},{2,0},{3,1},{4,6},{5,7},{6,4},{7,5},{8,10},{9,11},{10,... | collective-permute-start | bytes 393224 | tf_op jit(solution)/shard_map/ppermute | solution.py:247
  10.2 0.7 %compare_select_fusion.refs_0_ = s32[1,128]{1,0:T(1,128)S(1)} fusion(s32[1,1,128]{2,1,0:T(1,128)} %param.14, s32[1,1,128]{2,1,0:T(1,128)} %param.13, s32[]{:T(128)} %bitcast.6), kind=kLoop, calls=%fused_computation | loop fusion | flops 512 | bytes 1540 | tf_op jit(solution)/shard_map/jit(_where)/select_n | solution.py:265
  10.9 0.6 %collective-permute-start.4 = (bf16[256,128]{1,0:T(8,128)(2,1)S(1)}, bf16[256,128]{1,0:T(8,128)(2,1)S(1)}, u32[]{:S(2)}, u32[]{:S(2)}) collective-permute-start(bf16[256,128]{1,0:T(8,128)(2,1)S(1)} %collective-permute-done.3.refs_5_), channel_id=1, source_target_pairs={{0,4},{4,0},{8,12},{12,8},{16,20},{20,16},{24,28},{28,24},{1,5},{5... | collective-permute-start | bytes 196616 | tf_op jit(solution)/shard_map/ppermute | solution.py:247
  11.5 1.5 %collective-permute-start.2 = (bf16[256,128]{1,0:T(8,128)(2,1)S(1)}, bf16[256,128]{1,0:T(8,128)(2,1)S(1)}, u32[]{:S(2)}, u32[]{:S(2)}) collective-permute-start(bf16[256,128]{1,0:T(8,128)(2,1)S(1)} %collective-permute-done.1.refs_3_), channel_id=1, source_target_pairs={{0,4},{4,0},{8,12},{12,8},{16,20},{20,16},{24,28},{28,24},{1,5},{5... | collective-permute-start | bytes 196616 | tf_op jit(solution)/shard_map/ppermute | solution.py:247
  13.0 0.2 shard_map.111.refs_0_
  13.2 0.0 copy-start.4
  13.2 2.7 %shard_map.112.refs_0_ = bf16[1024,2048]{1,0:T(8,128)(2,1)S(1)} custom-call(s32[2,256]{1,0:T(2,128)S(1)} %shard_map.111.refs_0_, bf16[128,128,128]{2,1,0:T(8,128)(2,1)S(1)} %bitcast.7), custom_call_target="tpu_custom_call" | custom-call | bytes 8388608 | tf_op jit(solution)/shard_map/pallas_call | solution.py:35
  15.9 0.0 collective-permute-done.5.refs_7_
  15.9 0.5 %collective-permute-start.6 = (bf16[256,128]{1,0:T(8,128)(2,1)S(1)}, bf16[256,128]{1,0:T(8,128)(2,1)S(1)}, u32[]{:S(2)}, u32[]{:S(2)}) collective-permute-start(bf16[256,128]{1,0:T(8,128)(2,1)S(1)} %collective-permute-done.5.refs_7_), channel_id=1, source_target_pairs={{0,4},{4,0},{8,12},{12,8},{16,20},{20,16},{24,28},{28,24},{1,5},{5... | collective-permute-start | bytes 196616 | tf_op jit(solution)/shard_map/ppermute | solution.py:247
  16.5 1.1 %shard_map.113.refs_1_ = f32[1024,128]{1,0:T(8,128)S(1)} custom-call(bf16[1024,2048]{1,0:T(8,128)(2,1)S(1)} %shard_map.112.refs_0_, bf16[256,128]{1,0:T(8,128)(2,1)S(1)} %copy-done.4, bf16[256,128]{1,0:T(8,128)(2,1)S(1)} %collective-permute-done.refs_2_, bf16[256,128]{1,0:T(8,128)(2,1)S(1)} %collective-permute-done.1.refs_3_, ...), custom_call_target="tpu_custom_call" | custom-call | flops 34359738368 | bytes 4194304 | tf_op jit(solution)/shard_map/pallas_call | solution.py:35
  17.6 0.0 copy-start.1
  17.6 0.0 copy-start.2
  17.6 0.0 copy-start.3
  17.6 2.6 %collective-permute-done.6.refs_2_ = bf16[256,128]{1,0:T(8,128)(2,1)S(1)} collective-permute-done((bf16[256,128]{1,0:T(8,128)(2,1)S(1)}, bf16[256,128]{1,0:T(8,128)(2,1)S(1)}, u32[]{:S(2)}, u32[]{:S(2)}) %collective-permute-start.6) | collective-permute-done | bytes 65568 | tf_op jit(solution)/shard_map/ppermute | solution.py:247
  20.2 0.2 shard_map.115
  20.5 0.1 collective-permute-start.7
  20.5 0.2 shard_map.114.refs_0_
  20.8 1.1 %collective-permute-done.7.refs_1_ = bf16[512,128]{1,0:T(8,128)(2,1)S(1)} collective-permute-done((bf16[512,128]{1,0:T(8,128)(2,1)S(1)}, bf16[512,128]{1,0:T(8,128)(2,1)S(1)}, u32[]{:S(2)}, u32[]{:S(2)}) %collective-permute-start.7) | collective-permute-done | bytes 131104 | tf_op jit(solution)/shard_map/ppermute | solution.py:247
  21.9 0.4 collective-permute-start.9
  22.3 5.2 %collective-permute-done.9.refs_1_ = bf16[512,128]{1,0:T(8,128)(2,1)S(1)} collective-permute-done((bf16[512,128]{1,0:T(8,128)(2,1)S(1)}, bf16[512,128]{1,0:T(8,128)(2,1)S(1)}, u32[]{:S(2)}, u32[]{:S(2)}) %collective-permute-start.9) | collective-permute-done | bytes 131104 | tf_op jit(solution)/shard_map/ppermute | solution.py:247
  27.5 0.4 shard_map.117
  28.0 0.1 collective-permute-start.10
  28.1 0.3 shard_map.120
  28.3 0.6 %collective-permute-start.11 = (bf16[80,256]{1,0:T(8,128)(2,1)S(1)}, bf16[80,256]{1,0:T(8,128)(2,1)S(1)}, u32[]{:S(2)}, u32[]{:S(2)}) collective-permute-start(bf16[80,256]{1,0:T(8,128)(2,1)S(1)} %get-tuple-element.26), channel_id=1, source_target_pairs={{0,1},{1,0},{2,3},{3,2},{4,5},{5,4},{6,7},{7,6},{8,9},{9,8},{10,11... | collective-permute-start | bytes 122888 | tf_op jit(solution)/shard_map/ppermute | solution.py:247
  28.9 0.5 %collective-permute-done.10.refs_2_ = bf16[512,128]{1,0:T(8,128)(2,1)S(1)} collective-permute-done((bf16[512,128]{1,0:T(8,128)(2,1)S(1)}, bf16[512,128]{1,0:T(8,128)(2,1)S(1)}, u32[]{:S(2)}, u32[]{:S(2)}) %collective-permute-start.10) | collective-permute-done | bytes 131104 | tf_op jit(solution)/shard_map/ppermute | solution.py:247
  29.4 0.3 shard_map.118.refs_4_.refs_2_
  29.7 0.0 collective-permute-done.11.refs_1_
  29.8 0.5 collective-permute-start.12
  30.2 0.4 collective-permute-start.16
  30.7 3.2 %collective-permute-done.12.refs_1_ = bf16[80,256]{1,0:T(8,128)(2,1)S(1)} collective-permute-done((bf16[80,256]{1,0:T(8,128)(2,1)S(1)}, bf16[80,256]{1,0:T(8,128)(2,1)S(1)}, u32[]{:S(2)}, u32[]{:S(2)}) %collective-permute-start.12) | collective-permute-done | bytes 40992 | tf_op jit(solution)/shard_map/ppermute | solution.py:247
  33.9 0.3 shard_map.123
  34.2 0.5 collective-permute-start.13
  34.7 3.5 %collective-permute-start.14 = (bf16[80,256]{1,0:T(8,128)(2,1)S(1)}, bf16[80,256]{1,0:T(8,128)(2,1)S(1)}, u32[]{:S(2)}, u32[]{:S(2)}) collective-permute-start(bf16[80,256]{1,0:T(8,128)(2,1)S(1)} %shard_map.122.refs_3_.refs_0_), channel_id=1, source_target_pairs={{0,16},{4,20},{8,24},{12,28},{16,0},{20,4},{24,8},{28,12},{1,17},{... | collective-permute-start | bytes 122888 | tf_op jit(solution)/shard_map/ppermute | solution.py:247
  38.1 1.0 %shard_map.119 = (f32[4,128,256]{2,1,0:T(8,128)S(1)}, bf16[256,256]{1,0:T(8,128)(2,1)}) custom-call(bf16[1024,2048]{1,0:T(8,128)(2,1)S(1)} %shard_map.112.refs_0_, bf16[512,128]{1,0:T(8,128)(2,1)S(1)} %get-tuple-element.19.refs_1_, bf16[512,128]{1,0:T(8,128)(2,1)S(1)} %collective-permute-done.10.refs_2_, bf16[256,256]{1,0:T(8,128)(2,1)S(1)} %get-tuple-element.20.refs_3_, ...), custom_call_target="tpu_custom_call" | custom-call | flops 268435456 | bytes 2097152 | tf_op jit(solution)/shard_map/pallas_call | solution.py:35
  39.1 0.0 collective-permute-done.16.refs_1_
  39.2 0.1 collective-permute-start.17
  39.3 2.4 %collective-permute-start.18 = (bf16[128,256]{1,0:T(8,128)(2,1)S(1)}, bf16[128,256]{1,0:T(8,128)(2,1)S(1)}, u32[]{:S(2)}, u32[]{:S(2)}) collective-permute-start(bf16[128,256]{1,0:T(8,128)(2,1)S(1)} %get-tuple-element.28), channel_id=1, source_target_pairs={{0,24},{4,28},{8,16},{12,20},{16,8},{20,12},{24,0},{28,4},{1,25},{... | collective-permute-start | bytes 196616 | tf_op jit(solution)/shard_map/ppermute | solution.py:247
  41.7 0.0 collective-permute-done.14.refs_1_
  41.8 0.8 %collective-permute-start.15 = (bf16[208,256]{1,0:T(8,128)(2,1)S(1)}, bf16[208,256]{1,0:T(8,128)(2,1)S(1)}, u32[]{:S(2)}, u32[]{:S(2)}) collective-permute-start(bf16[208,256]{1,0:T(8,128)(2,1)S(1)} %shard_map.125), channel_id=1, source_target_pairs={{0,4},{4,0},{8,12},{12,8},{16,20},{20,16},{24,28},{28,24},{1,5},{5... | collective-permute-start | bytes 319496 | tf_op jit(solution)/shard_map/ppermute | solution.py:247
  42.6 3.5 %collective-permute-done.17.refs_0_ = bf16[128,256]{1,0:T(8,128)(2,1)S(1)} collective-permute-done((bf16[128,256]{1,0:T(8,128)(2,1)S(1)}, bf16[128,256]{1,0:T(8,128)(2,1)S(1)}, u32[]{:S(2)}, u32[]{:S(2)}) %collective-permute-start.17) | collective-permute-done | bytes 65568 | tf_op jit(solution)/shard_map/ppermute | solution.py:247
  46.1 0.4 collective-permute-done.15.refs_1_
  46.6 0.1 collective-permute-start.19
  46.7 1.2 %collective-permute-done.19.refs_2_ = f32[64,256]{1,0:T(8,128)S(1)} collective-permute-done((f32[64,256]{1,0:T(8,128)S(1)}, f32[64,256]{1,0:T(8,128)S(1)}, u32[]{:S(2)}, u32[]{:S(2)}) %collective-permute-start.19) | collective-permute-done | bytes 65568 | tf_op jit(solution)/shard_map/ppermute | solution.py:247
  47.9 0.7 %shard_map.131 = (bf16[256,128]{1,0:T(8,128)(2,1)}, f32[128,256]{1,0:T(8,128)}, f32[1,256]{1,0:T(1,128)}) custom-call(f32[128,256]{1,0:T(8,128)S(1)} %shard_map.129.refs_0_, f32[64,256]{1,0:T(8,128)S(1)} %get-tuple-element.29.refs_1_, f32[64,256]{1,0:T(8,128)S(1)} %collective-permute-done.19.refs_2_, f32[1,256]{1,0:T(1,128)S(1)} %get-tuple-element.30.refs_3_), custom_call_target="tpu_custom_call" | custom-call | bytes 524288 | tf_op jit(solution)/shard_map/pallas_call | solution.py:35
  (24 shorter events, 0.3 us)
Async XLA Ops:
  0.6 10.2 %collective-permute-start.3 = (bf16[256,128]{1,0:T(8,128)(2,1)}, bf16[256,128]{1,0:T(8,128)(2,1)S(1)}, u32[]{:S(2)}, u32[]{:S(2)}) collective-permute-start(bf16[256,128]{1,0:T(8,128)(2,1)} %refs_1_.1), channel_id=1, source_target_pairs={{0,16},{4,20},{8,24},{12,28},{16,0},{20,4},{24,8},{28,12},{1,17},{... | collective-permute-start | bytes 196616 | tf_op jit(solution)/shard_map/ppermute | solution.py:247
  4.7 6.7 %collective-permute-start.1 = (bf16[256,128]{1,0:T(8,128)(2,1)}, bf16[256,128]{1,0:T(8,128)(2,1)S(1)}, u32[]{:S(2)}, u32[]{:S(2)}) collective-permute-start(bf16[256,128]{1,0:T(8,128)(2,1)} %refs_1_.1), channel_id=1, source_target_pairs={{0,8},{4,12},{8,0},{12,4},{16,24},{20,28},{24,16},{28,20},{1,9},{5... | collective-permute-start | bytes 196616 | tf_op jit(solution)/shard_map/ppermute | solution.py:247
  6.3 10.1 %collective-permute-start = (bf16[256,128]{1,0:T(8,128)(2,1)}, bf16[256,128]{1,0:T(8,128)(2,1)S(1)}, u32[]{:S(2)}, u32[]{:S(2)}) collective-permute-start(bf16[256,128]{1,0:T(8,128)(2,1)} %refs_1_.1), channel_id=1, source_target_pairs={{0,4},{4,0},{8,12},{12,8},{16,20},{20,16},{24,28},{28,24},{1,5},{5... | collective-permute-start | bytes 196616 | tf_op jit(solution)/shard_map/ppermute | solution.py:247
  7.8 8.1 %collective-permute-start.5 = (bf16[256,128]{1,0:T(8,128)(2,1)}, bf16[256,128]{1,0:T(8,128)(2,1)S(1)}, u32[]{:S(2)}, u32[]{:S(2)}) collective-permute-start(bf16[256,128]{1,0:T(8,128)(2,1)} %refs_1_.1), channel_id=1, source_target_pairs={{0,24},{4,28},{8,16},{12,20},{16,8},{20,12},{24,0},{28,4},{1,25},{... | collective-permute-start | bytes 196616 | tf_op jit(solution)/shard_map/ppermute | solution.py:247
  8.1 12.7 %collective-permute-start.8 = (bf16[256,256]{1,0:T(8,128)(2,1)}, bf16[256,256]{1,0:T(8,128)(2,1)S(1)}, u32[]{:S(2)}, u32[]{:S(2)}) collective-permute-start(bf16[256,256]{1,0:T(8,128)(2,1)} %refs_4_.1), channel_id=1, source_target_pairs={{0,2},{1,3},{2,0},{3,1},{4,6},{5,7},{6,4},{7,5},{8,10},{9,11},{10,... | collective-permute-start | bytes 393224 | tf_op jit(solution)/shard_map/ppermute | solution.py:247
  10.9 2.3 %copy-start = (bf16[1,1,128,128,128]{4,3,2,1,0:T(8,128)(2,1)S(1)}, bf16[1,1,128,128,128]{4,3,2,1,0:T(8,128)(2,1)}, u32[]{:S(2)}) copy-start(bf16[1,1,128,128,128]{4,3,2,1,0:T(8,128)(2,1)} %param.12) | copy-start | bytes 12582916
  10.9 5.6 %collective-permute-start.4 = (bf16[256,128]{1,0:T(8,128)(2,1)S(1)}, bf16[256,128]{1,0:T(8,128)(2,1)S(1)}, u32[]{:S(2)}, u32[]{:S(2)}) collective-permute-start(bf16[256,128]{1,0:T(8,128)(2,1)S(1)} %collective-permute-done.3.refs_5_), channel_id=1, source_target_pairs={{0,4},{4,0},{8,12},{12,8},{16,20},{20,16},{24,28},{28,24},{1,5},{5... | collective-permute-start | bytes 196616 | tf_op jit(solution)/shard_map/ppermute | solution.py:247
  11.5 5.0 %collective-permute-start.2 = (bf16[256,128]{1,0:T(8,128)(2,1)S(1)}, bf16[256,128]{1,0:T(8,128)(2,1)S(1)}, u32[]{:S(2)}, u32[]{:S(2)}) collective-permute-start(bf16[256,128]{1,0:T(8,128)(2,1)S(1)} %collective-permute-done.1.refs_3_), channel_id=1, source_target_pairs={{0,4},{4,0},{8,12},{12,8},{16,20},{20,16},{24,28},{28,24},{1,5},{5... | collective-permute-start | bytes 196616 | tf_op jit(solution)/shard_map/ppermute | solution.py:247
  13.2 3.3 %copy-start.4 = (bf16[256,128]{1,0:T(8,128)(2,1)S(1)}, bf16[256,128]{1,0:T(8,128)(2,1)}, u32[]{:S(2)}) copy-start(bf16[256,128]{1,0:T(8,128)(2,1)} %refs_1_.1) | copy-start | bytes 196612
  15.9 4.3 %collective-permute-start.6 = (bf16[256,128]{1,0:T(8,128)(2,1)S(1)}, bf16[256,128]{1,0:T(8,128)(2,1)S(1)}, u32[]{:S(2)}, u32[]{:S(2)}) collective-permute-start(bf16[256,128]{1,0:T(8,128)(2,1)S(1)} %collective-permute-done.5.refs_7_), channel_id=1, source_target_pairs={{0,4},{4,0},{8,12},{12,8},{16,20},{20,16},{24,28},{28,24},{1,5},{5... | collective-permute-start | bytes 196616 | tf_op jit(solution)/shard_map/ppermute | solution.py:247
  17.6 9.9 %copy-start.1 = (bf16[256,256]{1,0:T(8,128)(2,1)S(1)}, bf16[256,256]{1,0:T(8,128)(2,1)}, u32[]{:S(2)}) copy-start(bf16[256,256]{1,0:T(8,128)(2,1)} %refs_4_.1) | copy-start | bytes 393220
  17.6 9.9 %copy-start.2 = (bf16[128,256]{1,0:T(8,128)(2,1)S(1)}, bf16[128,256]{1,0:T(8,128)(2,1)}, u32[]{:S(2)}) copy-start(bf16[128,256]{1,0:T(8,128)(2,1)} %refs_2_.1) | copy-start | bytes 196612
  17.6 9.9 %copy-start.3 = (f32[256]{0:T(256)S(1)}, f32[256]{0:T(256)}, u32[]{:S(2)}) copy-start(f32[256]{0:T(256)} %param.10) | copy-start | bytes 3076
  20.5 1.4 %collective-permute-start.7 = (bf16[512,128]{1,0:T(8,128)(2,1)S(1)}, bf16[512,128]{1,0:T(8,128)(2,1)S(1)}, u32[]{:S(2)}, u32[]{:S(2)}) collective-permute-start(bf16[512,128]{1,0:T(8,128)(2,1)S(1)} %shard_map.115), channel_id=1, source_target_pairs={{0,1},{1,0},{2,3},{3,2},{4,5},{5,4},{6,7},{7,6},{8,9},{9,8},{10,11... | collective-permute-start | bytes 393224 | tf_op jit(solution)/shard_map/ppermute | solution.py:247
  21.9 5.6 %collective-permute-start.9 = (bf16[512,128]{1,0:T(8,128)(2,1)S(1)}, bf16[512,128]{1,0:T(8,128)(2,1)S(1)}, u32[]{:S(2)}, u32[]{:S(2)}) collective-permute-start(bf16[512,128]{1,0:T(8,128)(2,1)S(1)} %shard_map.116.refs_0_), channel_id=1, source_target_pairs={{0,2},{1,3},{2,0},{3,1},{4,6},{5,7},{6,4},{7,5},{8,10},{9,11},{10,... | collective-permute-start | bytes 393224 | tf_op jit(solution)/shard_map/ppermute | solution.py:247
  28.0 1.4 %collective-permute-start.10 = (bf16[512,128]{1,0:T(8,128)(2,1)S(1)}, bf16[512,128]{1,0:T(8,128)(2,1)S(1)}, u32[]{:S(2)}, u32[]{:S(2)}) collective-permute-start(bf16[512,128]{1,0:T(8,128)(2,1)S(1)} %get-tuple-element.19.refs_1_), channel_id=1, source_target_pairs={{0,1},{1,0},{2,3},{3,2},{4,5},{5,4},{6,7},{7,6},{8,9},{9,8},{10,11... | collective-permute-start | bytes 393224 | tf_op jit(solution)/shard_map/ppermute | solution.py:247
  28.3 1.4 %collective-permute-start.11 = (bf16[80,256]{1,0:T(8,128)(2,1)S(1)}, bf16[80,256]{1,0:T(8,128)(2,1)S(1)}, u32[]{:S(2)}, u32[]{:S(2)}) collective-permute-start(bf16[80,256]{1,0:T(8,128)(2,1)S(1)} %get-tuple-element.26), channel_id=1, source_target_pairs={{0,1},{1,0},{2,3},{3,2},{4,5},{5,4},{6,7},{7,6},{8,9},{9,8},{10,11... | collective-permute-start | bytes 122888 | tf_op jit(solution)/shard_map/ppermute | solution.py:247
  29.8 4.1 %collective-permute-start.12 = (bf16[80,256]{1,0:T(8,128)(2,1)S(1)}, bf16[80,256]{1,0:T(8,128)(2,1)S(1)}, u32[]{:S(2)}, u32[]{:S(2)}) collective-permute-start(bf16[80,256]{1,0:T(8,128)(2,1)S(1)} %shard_map.121.refs_0_), channel_id=1, source_target_pairs={{0,8},{4,12},{8,0},{12,4},{16,24},{20,28},{24,16},{28,20},{1,9},{5... | collective-permute-start | bytes 122888 | tf_op jit(solution)/shard_map/ppermute | solution.py:247
  30.2 8.9 %collective-permute-start.16 = (bf16[2,128,256]{2,1,0:T(8,128)(2,1)S(1)}, bf16[2,128,256]{2,1,0:T(8,128)(2,1)S(1)}, u32[]{:S(2)}, u32[]{:S(2)}) collective-permute-start(bf16[2,128,256]{2,1,0:T(8,128)(2,1)S(1)} %shard_map.118.refs_4_.refs_2_), channel_id=1, source_target_pairs={{0,4},{4,0},{8,12},{12,8},{16,20},{20,16},{24,28},{28,24},{1,5},{5... | collective-permute-start | bytes 393224 | tf_op jit(solution)/shard_map/ppermute | solution.py:247
  34.2 7.5 %collective-permute-start.13 = (bf16[2,128,256]{2,1,0:T(8,128)(2,1)S(1)}, bf16[2,128,256]{2,1,0:T(8,128)(2,1)S(1)}, u32[]{:S(2)}, u32[]{:S(2)}) collective-permute-start(bf16[2,128,256]{2,1,0:T(8,128)(2,1)S(1)} %shard_map.123), channel_id=1, source_target_pairs={{0,8},{4,12},{8,0},{12,4},{16,24},{20,28},{24,16},{28,20},{1,9},{5... | collective-permute-start | bytes 393224 | tf_op jit(solution)/shard_map/ppermute | solution.py:247
  34.7 7.0 %collective-permute-start.14 = (bf16[80,256]{1,0:T(8,128)(2,1)S(1)}, bf16[80,256]{1,0:T(8,128)(2,1)S(1)}, u32[]{:S(2)}, u32[]{:S(2)}) collective-permute-start(bf16[80,256]{1,0:T(8,128)(2,1)S(1)} %shard_map.122.refs_3_.refs_0_), channel_id=1, source_target_pairs={{0,16},{4,20},{8,24},{12,28},{16,0},{20,4},{24,8},{28,12},{1,17},{... | collective-permute-start | bytes 122888 | tf_op jit(solution)/shard_map/ppermute | solution.py:247
  39.2 6.9 %collective-permute-start.17 = (bf16[128,256]{1,0:T(8,128)(2,1)S(1)}, bf16[128,256]{1,0:T(8,128)(2,1)S(1)}, u32[]{:S(2)}, u32[]{:S(2)}) collective-permute-start(bf16[128,256]{1,0:T(8,128)(2,1)S(1)} %get-tuple-element.27), channel_id=1, source_target_pairs={{0,16},{4,20},{8,24},{12,28},{16,0},{20,4},{24,8},{28,12},{1,17},{... | collective-permute-start | bytes 196616 | tf_op jit(solution)/shard_map/ppermute | solution.py:247
  39.3 6.8 %collective-permute-start.18 = (bf16[128,256]{1,0:T(8,128)(2,1)S(1)}, bf16[128,256]{1,0:T(8,128)(2,1)S(1)}, u32[]{:S(2)}, u32[]{:S(2)}) collective-permute-start(bf16[128,256]{1,0:T(8,128)(2,1)S(1)} %get-tuple-element.28), channel_id=1, source_target_pairs={{0,24},{4,28},{8,16},{12,20},{16,8},{20,12},{24,0},{28,4},{1,25},{... | collective-permute-start | bytes 196616 | tf_op jit(solution)/shard_map/ppermute | solution.py:247
  41.8 4.8 %collective-permute-start.15 = (bf16[208,256]{1,0:T(8,128)(2,1)S(1)}, bf16[208,256]{1,0:T(8,128)(2,1)S(1)}, u32[]{:S(2)}, u32[]{:S(2)}) collective-permute-start(bf16[208,256]{1,0:T(8,128)(2,1)S(1)} %shard_map.125), channel_id=1, source_target_pairs={{0,4},{4,0},{8,12},{12,8},{16,20},{20,16},{24,28},{28,24},{1,5},{5... | collective-permute-start | bytes 319496 | tf_op jit(solution)/shard_map/ppermute | solution.py:247
  46.6 1.3 %collective-permute-start.19 = (f32[64,256]{1,0:T(8,128)S(1)}, f32[64,256]{1,0:T(8,128)S(1)}, u32[]{:S(2)}, u32[]{:S(2)}) collective-permute-start(f32[64,256]{1,0:T(8,128)S(1)} %get-tuple-element.29.refs_1_), channel_id=1, source_target_pairs={{0,1},{1,0},{2,3},{3,2},{4,5},{5,4},{6,7},{7,6},{8,9},{9,8},{10,11... | collective-permute-start | bytes 196616 | tf_op jit(solution)/shard_map/ppermute | solution.py:247

commit v2 on v1

--- a/solution.py
+++ b/solution.py
@@ -35,9 +35,13 @@
     return lambda *args: run(*args, *after)
 
 
-def lists_kernel(places, lists):
-    slots, wide = places.shape[1], lists.shape[1]
-    by_slot = jnp.broadcast_to(places[...].astype(F32), (slots, slots))
+def relay_kernel(source, target):
+    target[...] = source[...]
+
+
+def lists_kernel(col_tiles, rows, cols, lists):
+    slots, wide = rows.shape[2], lists.shape[1]
+    by_slot = jnp.broadcast_to((rows[0] * col_tiles + cols[0]).astype(F32), (slots, slots))
     down = by_slot.T[:, :1]
     slot = lax.broadcasted_iota(jnp.int32, (slots, wide), 0)
     at = lax.broadcasted_iota(jnp.int32, (slots, wide), 1)
@@ -50,20 +54,21 @@
     lists[1:2, slots:] = jnp.full((1, wide - slots), slots, jnp.int32)
 
 
-def densify_kernel(lists, values, dense, head, after, many, list_sems):
+def densify_kernel(lists, count, values, dense, head, after, many, sems):
     slots, tile, _ = values.shape
     row_tiles, col_tiles = dense.shape[0] // tile, dense.shape[1] // tile
     moves = [
-        pltpu.make_async_copy(lists.at[pl.ds(0, 1)], head, list_sems.at[0]),
-        pltpu.make_async_copy(lists.at[pl.ds(1, 1)], after, list_sems.at[1]),
+        pltpu.make_async_copy(lists.at[pl.ds(0, 1)], head, sems.at[0]),
+        pltpu.make_async_copy(lists.at[pl.ds(1, 1)], after, sems.at[1]),
     ]
     for copy in moves:
         copy.start()
     for copy in moves:
         copy.wait()
+    end = count[0, 0]
 
     def held(slot):
-        return jnp.where(slot < slots, values[jnp.minimum(slot, slots - 1)], 0)
+        return jnp.where(slot < end, values[jnp.minimum(slot, slots - 1)], 0)
 
     def write(row, found):
         top = pl.ds(pl.multiple_of(row * tile, tile), tile)
@@ -73,7 +78,7 @@
             two = after[0, one]
             dense[top, col * tile : (col + 1) * tile] = held(one) + held(two)
             many[found] = place
-            found += (after[0, two] < slots).astype(jnp.int32)
+            found += (after[0, two] < end).astype(jnp.int32)
         return found
 
     found = lax.fori_loop(0, row_tiles, write, jnp.int32(0))
@@ -88,37 +93,27 @@
             slot, total = state
             return after[0, slot], total + values[slot].astype(F32)
 
-        _, total = lax.while_loop(
-            lambda state: state[0] < slots, more, (head[0, place], jnp.zeros((tile, tile), F32))
-        )
+        one = head[0, place]
+        two = after[0, one]
+        three = after[0, two]
+        total = values[one].astype(F32) + values[two].astype(F32) + values[three].astype(F32)
+        _, total = lax.while_loop(lambda state: state[0] < end, more, (after[0, three], total))
         dense[top, left] = total.astype(BF16)
         return carry
 
     lax.fori_loop(0, found, rewrite, 0)
 
 
-def forward_kernel(dense, own, y_1, near, y_near, far_4, y_4, far_6, out):
-    pieces = (own, y_1, near, y_near, far_4, y_4, far_6)
-    nodes = own.shape[0]
+def forward_kernel(places, dense, *refs):
+    pieces, out = refs[:-1], refs[-1]
+    nodes = pieces[0].shape[0]
     r, c = lax.axis_index("row"), lax.axis_index("col")
-    for at, j in enumerate((1, 3, 0, 2)):
+    for at, j in enumerate(places):
         top = pl.ds(pl.multiple_of((c ^ j) * nodes, nodes), nodes)
-        acc = jnp.zeros(own.shape, F32)
+        acc = jnp.zeros(pieces[0].shape, F32)
         for i, piece in enumerate(pieces):
             left = pl.ds(pl.multiple_of((r ^ i) * nodes, nodes), nodes)
             acc += jnp.dot(dense[top, left], piece[...], preferred_element_type=F32)
-        out[at * nodes : (at + 1) * nodes, :] = acc
-
-
-def finish_kernel(start, dense, most, y_6, out):
-    nodes = y_6.shape[0]
-    r, c = lax.axis_index("row"), lax.axis_index("col")
-    left = pl.ds(pl.multiple_of((r ^ 7) * nodes, nodes), nodes)
-    for at in range(2):
-        j = (1, 3, 0, 2)[start + at]
-        top = pl.ds(pl.multiple_of((c ^ j) * nodes, nodes), nodes)
-        acc = most[(start + at) * nodes : (start + at + 1) * nodes, :]
-        acc += jnp.dot(dense[top, left], y_6[...], preferred_element_type=F32)
         out[at * nodes : (at + 1) * nodes, :] = acc.astype(out.dtype)
 
 
@@ -258,21 +253,18 @@
     shape = jax.ShapeDtypeStruct
 
     far = [swap(features, "row", 4), swap(features, "row", 6)]
-    near = swap(features, "row", 2)
+    near = call(relay_kernel, shape(features.shape, BF16), [IN_VMEM], flops=FIRST)(swap(features, "row", 2))
     grad_out_x = swap(grad_out, "col", 2)
     y_1, y_near = swap(features, "row", 1), swap(near, "row", 1)
     y_4, y_6 = swap(far[0], "row", 1), swap(far[1], "row", 1)
-    places = jnp.where(
-        jnp.arange(slots, dtype=jnp.int32) < tile_count[0, 0],
-        tile_rows[0, 0] * (length // tile) + tile_cols[0, 0],
-        positions,
-    ).reshape(1, slots)
     wide = 128 * pl.cdiv(max(positions, slots + 1), 128)
-    lists = call(lists_kernel, shape((2, wide), jnp.int32), [IN_VMEM], flops=FIRST)(places)
+    lists = call(
+        functools.partial(lists_kernel, length // tile), shape((2, wide), jnp.int32), [IN_VMEM] * 2
+    )(tile_rows, tile_cols)
     dense = call(
         densify_kernel,
         shape((height, length), BF16),
-        [IN_VMEM] * 2,
+        [IN_VMEM, pl.BlockSpec(memory_space=pltpu.SMEM), IN_VMEM],
         [
             pltpu.SMEM((1, wide), jnp.int32),
             pltpu.SMEM((1, wide), jnp.int32),
@@ -280,32 +272,24 @@
             pltpu.SemaphoreType.DMA((2,)),
         ],
         nbytes=2 * tile_values.size * 2,
-    )(lists, tile_values.reshape(slots, tile, tile))
-    most = call(
-        forward_kernel,
-        shape((4 * nodes, width_in), F32),
-        [IN_VMEM] * 8,
-        flops=FIRST,
-        nbytes=2 * height * length,
-    )(dense, features, y_1, near, y_near, far[0], y_4, far[1])
-
-    def finish(start, dtype):
+    )(lists, tile_count, tile_values.reshape(slots, tile, tile))
+    def forward(parts, dtype):
         return call(
-            functools.partial(finish_kernel, start),
+            functools.partial(forward_kernel, parts),
             shape((2 * nodes, width_in), dtype),
-            [IN_VMEM] * 3,
-            flops=whole // 16,
-            nbytes=height * length // 8,
-        )(dense, most, y_6)
-
-    core_share = swap(finish(0, BF16), "col", 1)
+            [IN_VMEM] * (1 + n_row),
+            flops=whole // 2,
+            nbytes=height * length,
+        )(dense, features, y_1, near, y_near, far[0], y_4, far[1], y_6)
+
+    core_share = swap(forward((1, 3), BF16), "col", 1)
     half = call(
         add_kernel,
         shape((2 * nodes, width_in), BF16),
         [IN_VMEM] * 2,
         nbytes=16 * nodes * width_in,
         after=[grad_out_x],
-    )(finish(2, F32), core_share)
+    )(forward((0, 2), F32), core_share)
     half_x = swap(half, "col", 2)
     aggregate, grad_pre, hidden, grad_aggregate = call(
         layer_kernel,
@@ -365,7 +349,7 @@
         )(own, other)
 
     part = merge(mine, swap(theirs, "col", 1), [sent_far])
-    part = merge(part, swap(part, "row", 2))
+    part = merge(part, swap(part, "row", 2), [kept])
     sent_near = backward((2, 3), BF16, [part])
     arrived_near = swap(sent_near, "row", 2)
     part = merge(part, swap(part, "row", 4))

time: 48.9 us -> 46.7 us (0.955)
  waiting for transfers between devices: 17.8 us -> 16.1 us
  other arithmetic: 0.68 us -> 0 us
  starting transfers between devices: 20.9 us -> 21.4 us
    ppermute x20, waiting for transfers between devices: 17.8 us -> 16.1 us  [swap(): return lax.ppermute(value, axis, [(at, at ^ bits) for at in range(size)])]
    select_n x1 -> x0, other arithmetic: 0.68 us -> none  [dense_block(): jnp.where(jnp.arange(slots, dtype=jnp.int32) < tile_count[0, 0], tile_row...]
    ppermute x20, starting transfers between devices: 20.9 us -> 21.4 us  [swap(): return lax.ppermute(value, axis, [(at, at ^ bits) for at in range(size)])]
  transfers between devices with their start and end apart: 20 -> 20, of which waited for: 8 -> 7; matrix products, arithmetic and copies ran while one was open for 1% -> 0% of each run, Pallas kernels for 13% -> 13%
where the time goes in v2:
time: 46.7 us; the launch traced here: 46.5 us
  starting transfers between devices  21.4 us (46%)
  waiting for transfers between devices  16.1 us (34%)
  Pallas kernels  7.41 us (16%)
  between operations  1.57 us (3%)
    ppermute x20, starting transfers between devices, swap(): return lax.ppermute(value, axis, [(at, at ^ bits) for at in range(size)])  21.4 us
    ppermute x20, waiting for transfers between devices, swap(): return lax.ppermute(value, axis, [(at, at ^ bits) for at in range(size)])  16.1 us
    pallas_call x21, Pallas kernels, call(): return lambda *args: run(*args, *after)  7.41 us
  transfers between devices with their start and end apart: 20, of which 7 were waited for; matrix products, arithmetic and copies ran while one was open for 0% of the time, Pallas kernels for 13%

profile of v2, /device:TPU:0, one launch (start us, length us, event | category | flops | bytes accessed | tf_op | source)
XLA Modules:
  0.0 46.5 jit_solution(7659516899224278270)
XLA Ops:
  0.7 3.1 %collective-permute-start.1 = (bf16[256,128]{1,0:T(8,128)(2,1)}, bf16[256,128]{1,0:T(8,128)(2,1)S(1)}, u32[]{:S(2)}, u32[]{:S(2)}) collective-permute-start(bf16[256,128]{1,0:T(8,128)(2,1)} %refs_1_.6), channel_id=1, source_target_pairs={{0,8},{4,12},{8,0},{12,4},{16,24},{20,28},{24,16},{28,20},{1,9},{5... | collective-permute-start | bytes 196616 | tf_op jit(solution)/shard_map/ppermute | solution.py:242
  3.8 2.6 %collective-permute-start.3 = (bf16[256,128]{1,0:T(8,128)(2,1)}, bf16[256,128]{1,0:T(8,128)(2,1)S(1)}, u32[]{:S(2)}, u32[]{:S(2)}) collective-permute-start(bf16[256,128]{1,0:T(8,128)(2,1)} %refs_1_.6), channel_id=1, source_target_pairs={{0,16},{4,20},{8,24},{12,28},{16,0},{20,4},{24,8},{28,12},{1,17},{... | collective-permute-start | bytes 196616 | tf_op jit(solution)/shard_map/ppermute | solution.py:242
  6.4 0.0 collective-permute-start.5
  6.4 1.7 %collective-permute-start = (bf16[256,128]{1,0:T(8,128)(2,1)}, bf16[256,128]{1,0:T(8,128)(2,1)S(1)}, u32[]{:S(2)}, u32[]{:S(2)}) collective-permute-start(bf16[256,128]{1,0:T(8,128)(2,1)} %refs_1_.6), channel_id=1, source_target_pairs={{0,4},{4,0},{8,12},{12,8},{16,20},{20,16},{24,28},{28,24},{1,5},{5... | collective-permute-start | bytes 196616 | tf_op jit(solution)/shard_map/ppermute | solution.py:242
  8.1 0.4 collective-permute-start.2
  8.5 2.8 %collective-permute-done.3.refs_5_ = bf16[256,128]{1,0:T(8,128)(2,1)S(1)} collective-permute-done((bf16[256,128]{1,0:T(8,128)(2,1)}, bf16[256,128]{1,0:T(8,128)(2,1)S(1)}, u32[]{:S(2)}, u32[]{:S(2)}) %collective-permute-start.3) | collective-permute-done | bytes 65568 | tf_op jit(solution)/shard_map/ppermute | solution.py:242
  11.3 1.5 %collective-permute-start.4 = (bf16[256,128]{1,0:T(8,128)(2,1)S(1)}, bf16[256,128]{1,0:T(8,128)(2,1)S(1)}, u32[]{:S(2)}, u32[]{:S(2)}) collective-permute-start(bf16[256,128]{1,0:T(8,128)(2,1)S(1)} %collective-permute-done.3.refs_5_), channel_id=1, source_target_pairs={{0,4},{4,0},{8,12},{12,8},{16,20},{20,16},{24,28},{28,24},{1,5},{5... | collective-permute-start | bytes 196616 | tf_op jit(solution)/shard_map/ppermute | solution.py:242
  12.8 0.0 collective-permute-done.5.refs_7_
  12.8 1.4 %collective-permute-start.6 = (bf16[256,128]{1,0:T(8,128)(2,1)S(1)}, bf16[256,128]{1,0:T(8,128)(2,1)S(1)}, u32[]{:S(2)}, u32[]{:S(2)}) collective-permute-start(bf16[256,128]{1,0:T(8,128)(2,1)S(1)} %collective-permute-done.5.refs_7_), channel_id=1, source_target_pairs={{0,4},{4,0},{8,12},{12,8},{16,20},{20,16},{24,28},{28,24},{1,5},{5... | collective-permute-start | bytes 196616 | tf_op jit(solution)/shard_map/ppermute | solution.py:242
  14.2 1.5 %collective-permute-start.8 = (bf16[256,256]{1,0:T(8,128)(2,1)S(1)}, bf16[256,256]{1,0:T(8,128)(2,1)S(1)}, u32[]{:S(2)}, u32[]{:S(2)}) collective-permute-start(bf16[256,256]{1,0:T(8,128)(2,1)S(1)} %copy-done.2), channel_id=1, source_target_pairs={{0,2},{1,3},{2,0},{3,1},{4,6},{5,7},{6,4},{7,5},{8,10},{9,11},{10,... | collective-permute-start | bytes 393224 | tf_op jit(solution)/shard_map/ppermute | solution.py:242
  16.3 0.2 shard_map.111.refs_0_
  16.5 0.0 copy-start.1
  16.5 2.5 %shard_map.112.refs_0_ = bf16[1024,2048]{1,0:T(8,128)(2,1)S(1)} custom-call(s32[2,256]{1,0:T(2,128)S(1)} %shard_map.111.refs_0_, s32[1,1]{1,0:T(1,128)S(6)} %copy.12.refs_1_, bf16[128,128,128]{2,1,0:T(8,128)(2,1)S(1)} %bitcast.3), custom_call_target="tpu_custom_call" | custom-call | bytes 8388608 | tf_op jit(solution)/shard_map/pallas_call | solution.py:35
  19.0 0.0 copy-start.3
  19.0 0.0 copy-start.4
  19.1 0.0 collective-permute-done.refs_2_
  19.1 0.0 collective-permute-done.4.refs_6_
  19.1 0.0 collective-permute-done.6.refs_8_
  19.1 0.7 %shard_map.115 = bf16[512,128]{1,0:T(8,128)(2,1)S(1)} custom-call(bf16[1024,2048]{1,0:T(8,128)(2,1)S(1)} %shard_map.112.refs_0_, bf16[256,128]{1,0:T(8,128)(2,1)S(1)} %copy-done.1, bf16[256,128]{1,0:T(8,128)(2,1)S(1)} %collective-permute-done.refs_2_, bf16[256,128]{1,0:T(8,128)(2,1)S(1)} %shard_map.113.refs_3_, ...), custom_call_target="tpu_custom_call" | custom-call | flops 268435456 | bytes 2097152 | tf_op jit(solution)/shard_map/pallas_call | solution.py:35
  19.8 0.1 collective-permute-start.7
  19.9 0.7 %shard_map.114.refs_0_ = f32[512,128]{1,0:T(8,128)S(1)} custom-call(bf16[1024,2048]{1,0:T(8,128)(2,1)S(1)} %shard_map.112.refs_0_, bf16[256,128]{1,0:T(8,128)(2,1)S(1)} %copy-done.1, bf16[256,128]{1,0:T(8,128)(2,1)S(1)} %collective-permute-done.refs_2_, bf16[256,128]{1,0:T(8,128)(2,1)S(1)} %shard_map.113.refs_3_, ...), custom_call_target="tpu_custom_call" | custom-call | flops 268435456 | bytes 2097152 | tf_op jit(solution)/shard_map/pallas_call | solution.py:35
  20.6 0.0 collective-permute-done.8.refs_2_.refs_5_
  20.6 0.6 %collective-permute-done.7.refs_1_ = bf16[512,128]{1,0:T(8,128)(2,1)S(1)} collective-permute-done((bf16[512,128]{1,0:T(8,128)(2,1)S(1)}, bf16[512,128]{1,0:T(8,128)(2,1)S(1)}, u32[]{:S(2)}, u32[]{:S(2)}) %collective-permute-start.7) | collective-permute-done | bytes 131104 | tf_op jit(solution)/shard_map/ppermute | solution.py:242
  21.3 0.5 %collective-permute-start.9 = (bf16[512,128]{1,0:T(8,128)(2,1)S(1)}, bf16[512,128]{1,0:T(8,128)(2,1)S(1)}, u32[]{:S(2)}, u32[]{:S(2)}) collective-permute-start(bf16[512,128]{1,0:T(8,128)(2,1)S(1)} %shard_map.116.refs_0_), channel_id=1, source_target_pairs={{0,2},{1,3},{2,0},{3,1},{4,6},{5,7},{6,4},{7,5},{8,10},{9,11},{10,... | collective-permute-start | bytes 393224 | tf_op jit(solution)/shard_map/ppermute | solution.py:242
  21.8 5.1 %collective-permute-done.9.refs_1_ = bf16[512,128]{1,0:T(8,128)(2,1)S(1)} collective-permute-done((bf16[512,128]{1,0:T(8,128)(2,1)S(1)}, bf16[512,128]{1,0:T(8,128)(2,1)S(1)}, u32[]{:S(2)}, u32[]{:S(2)}) %collective-permute-start.9) | collective-permute-done | bytes 131104 | tf_op jit(solution)/shard_map/ppermute | solution.py:242
  26.9 0.4 shard_map.117
  27.3 0.1 collective-permute-start.10
  27.4 0.3 shard_map.120
  27.7 0.6 %collective-permute-start.11 = (bf16[80,256]{1,0:T(8,128)(2,1)S(1)}, bf16[80,256]{1,0:T(8,128)(2,1)S(1)}, u32[]{:S(2)}, u32[]{:S(2)}) collective-permute-start(bf16[80,256]{1,0:T(8,128)(2,1)S(1)} %get-tuple-element.26), channel_id=1, source_target_pairs={{0,1},{1,0},{2,3},{3,2},{4,5},{5,4},{6,7},{7,6},{8,9},{9,8},{10,11... | collective-permute-start | bytes 122888 | tf_op jit(solution)/shard_map/ppermute | solution.py:242
  28.2 0.5 %collective-permute-done.10.refs_2_ = bf16[512,128]{1,0:T(8,128)(2,1)S(1)} collective-permute-done((bf16[512,128]{1,0:T(8,128)(2,1)S(1)}, bf16[512,128]{1,0:T(8,128)(2,1)S(1)}, u32[]{:S(2)}, u32[]{:S(2)}) %collective-permute-start.10) | collective-permute-done | bytes 131104 | tf_op jit(solution)/shard_map/ppermute | solution.py:242
  28.8 0.3 shard_map.118.refs_4_.refs_2_
  29.1 0.0 collective-permute-done.11.refs_1_
  29.1 0.1 collective-permute-start.12
  29.2 0.9 %collective-permute-start.16 = (bf16[2,128,256]{2,1,0:T(8,128)(2,1)S(1)}, bf16[2,128,256]{2,1,0:T(8,128)(2,1)S(1)}, u32[]{:S(2)}, u32[]{:S(2)}) collective-permute-start(bf16[2,128,256]{2,1,0:T(8,128)(2,1)S(1)} %shard_map.118.refs_4_.refs_2_), channel_id=1, source_target_pairs={{0,4},{4,0},{8,12},{12,8},{16,20},{20,16},{24,28},{28,24},{1,5},{5... | collective-permute-start | bytes 393224 | tf_op jit(solution)/shard_map/ppermute | solution.py:242
  30.1 1.0 %shard_map.119 = (f32[4,128,256]{2,1,0:T(8,128)S(1)}, bf16[256,256]{1,0:T(8,128)(2,1)}) custom-call(bf16[1024,2048]{1,0:T(8,128)(2,1)S(1)} %shard_map.112.refs_0_, bf16[512,128]{1,0:T(8,128)(2,1)S(1)} %get-tuple-element.19.refs_1_, bf16[512,128]{1,0:T(8,128)(2,1)S(1)} %collective-permute-done.10.refs_2_, bf16[256,256]{1,0:T(8,128)(2,1)S(1)} %get-tuple-element.20.refs_3_, ...), custom_call_target="tpu_custom_call" | custom-call | flops 268435456 | bytes 2097152 | tf_op jit(solution)/shard_map/pallas_call | solution.py:35
  31.1 2.1 %collective-permute-done.12.refs_1_ = bf16[80,256]{1,0:T(8,128)(2,1)S(1)} collective-permute-done((bf16[80,256]{1,0:T(8,128)(2,1)S(1)}, bf16[80,256]{1,0:T(8,128)(2,1)S(1)}, u32[]{:S(2)}, u32[]{:S(2)}) %collective-permute-start.12) | collective-permute-done | bytes 40992 | tf_op jit(solution)/shard_map/ppermute | solution.py:242
  33.2 0.3 shard_map.123
  33.6 0.2 collective-permute-start.13
  33.7 2.6 %collective-permute-start.14 = (bf16[80,256]{1,0:T(8,128)(2,1)S(1)}, bf16[80,256]{1,0:T(8,128)(2,1)S(1)}, u32[]{:S(2)}, u32[]{:S(2)}) collective-permute-start(bf16[80,256]{1,0:T(8,128)(2,1)S(1)} %shard_map.122.refs_3_.refs_0_), channel_id=1, source_target_pairs={{0,16},{4,20},{8,24},{12,28},{16,0},{20,4},{24,8},{28,12},{1,17},{... | collective-permute-start | bytes 122888 | tf_op jit(solution)/shard_map/ppermute | solution.py:242
  36.4 1.1 %collective-permute-start.17 = (bf16[128,256]{1,0:T(8,128)(2,1)S(1)}, bf16[128,256]{1,0:T(8,128)(2,1)S(1)}, u32[]{:S(2)}, u32[]{:S(2)}) collective-permute-start(bf16[128,256]{1,0:T(8,128)(2,1)S(1)} %get-tuple-element.27), channel_id=1, source_target_pairs={{0,16},{4,20},{8,24},{12,28},{16,0},{20,4},{24,8},{28,12},{1,17},{... | collective-permute-start | bytes 196616 | tf_op jit(solution)/shard_map/ppermute | solution.py:242
  37.5 2.1 %collective-permute-start.18 = (bf16[128,256]{1,0:T(8,128)(2,1)S(1)}, bf16[128,256]{1,0:T(8,128)(2,1)S(1)}, u32[]{:S(2)}, u32[]{:S(2)}) collective-permute-start(bf16[128,256]{1,0:T(8,128)(2,1)S(1)} %get-tuple-element.28), channel_id=1, source_target_pairs={{0,24},{4,28},{8,16},{12,20},{16,8},{20,12},{24,0},{28,4},{1,25},{... | collective-permute-start | bytes 196616 | tf_op jit(solution)/shard_map/ppermute | solution.py:242
  39.6 0.0 collective-permute-done.14.refs_1_
  39.6 1.0 %collective-permute-start.15 = (bf16[208,256]{1,0:T(8,128)(2,1)S(1)}, bf16[208,256]{1,0:T(8,128)(2,1)S(1)}, u32[]{:S(2)}, u32[]{:S(2)}) collective-permute-start(bf16[208,256]{1,0:T(8,128)(2,1)S(1)} %shard_map.125), channel_id=1, source_target_pairs={{0,4},{4,0},{8,12},{12,8},{16,20},{20,16},{24,28},{28,24},{1,5},{5... | collective-permute-start | bytes 319496 | tf_op jit(solution)/shard_map/ppermute | solution.py:242
  40.6 3.8 %collective-permute-done.17.refs_0_ = bf16[128,256]{1,0:T(8,128)(2,1)S(1)} collective-permute-done((bf16[128,256]{1,0:T(8,128)(2,1)S(1)}, bf16[128,256]{1,0:T(8,128)(2,1)S(1)}, u32[]{:S(2)}, u32[]{:S(2)}) %collective-permute-start.17) | collective-permute-done | bytes 65568 | tf_op jit(solution)/shard_map/ppermute | solution.py:242
  44.4 0.0 collective-permute-done.18.refs_1_
  44.5 0.1 collective-permute-start.19
  44.6 1.2 %collective-permute-done.19.refs_2_ = f32[64,256]{1,0:T(8,128)S(1)} collective-permute-done((f32[64,256]{1,0:T(8,128)S(1)}, f32[64,256]{1,0:T(8,128)S(1)}, u32[]{:S(2)}, u32[]{:S(2)}) %collective-permute-start.19) | collective-permute-done | bytes 65568 | tf_op jit(solution)/shard_map/ppermute | solution.py:242
  45.8 0.7 %shard_map.131 = (bf16[256,128]{1,0:T(8,128)(2,1)}, f32[128,256]{1,0:T(8,128)}, f32[1,256]{1,0:T(1,128)}) custom-call(f32[128,256]{1,0:T(8,128)S(1)} %shard_map.129.refs_0_, f32[64,256]{1,0:T(8,128)S(1)} %get-tuple-element.29.refs_1_, f32[64,256]{1,0:T(8,128)S(1)} %collective-permute-done.19.refs_2_, f32[1,256]{1,0:T(1,128)S(1)} %get-tuple-element.30.refs_3_), custom_call_target="tpu_custom_call" | custom-call | bytes 524288 | tf_op jit(solution)/shard_map/pallas_call | solution.py:35
  (27 shorter events, 0.3 us)
Async XLA Ops:
  0.6 13.5 %copy-start.2 = (bf16[256,256]{1,0:T(8,128)(2,1)S(1)}, bf16[256,256]{1,0:T(8,128)(2,1)}, u32[]{:S(2)}) copy-start(bf16[256,256]{1,0:T(8,128)(2,1)} %refs_4_.1) | copy-start | bytes 393220
  0.6 15.7 %copy-start.5 = (s32[1,1,128]{2,1,0:T(1,128)S(1)}, s32[1,1,128]{2,1,0:T(1,128)}, u32[]{:S(2)}) copy-start(s32[1,1,128]{2,1,0:T(1,128)} %refs_0_.1) | copy-start | bytes 1540
  0.7 15.7 %copy-start.6 = (s32[1,1,128]{2,1,0:T(1,128)S(1)}, s32[1,1,128]{2,1,0:T(1,128)}, u32[]{:S(2)}) copy-start(s32[1,1,128]{2,1,0:T(1,128)} %refs_1_.4) | copy-start | bytes 1540
  0.7 15.9 %copy-start = (bf16[1,1,128,128,128]{4,3,2,1,0:T(8,128)(2,1)S(1)}, bf16[1,1,128,128,128]{4,3,2,1,0:T(8,128)(2,1)}, u32[]{:S(2)}) copy-start(bf16[1,1,128,128,128]{4,3,2,1,0:T(8,128)(2,1)} %param.12) | copy-start | bytes 12582916
  0.7 7.4 %collective-permute-start.1 = (bf16[256,128]{1,0:T(8,128)(2,1)}, bf16[256,128]{1,0:T(8,128)(2,1)S(1)}, u32[]{:S(2)}, u32[]{:S(2)}) collective-permute-start(bf16[256,128]{1,0:T(8,128)(2,1)} %refs_1_.6), channel_id=1, source_target_pairs={{0,8},{4,12},{8,0},{12,4},{16,24},{20,28},{24,16},{28,20},{1,9},{5... | collective-permute-start | bytes 196616 | tf_op jit(solution)/shard_map/ppermute | solution.py:242
  3.8 7.5 %collective-permute-start.3 = (bf16[256,128]{1,0:T(8,128)(2,1)}, bf16[256,128]{1,0:T(8,128)(2,1)S(1)}, u32[]{:S(2)}, u32[]{:S(2)}) collective-permute-start(bf16[256,128]{1,0:T(8,128)(2,1)} %refs_1_.6), channel_id=1, source_target_pairs={{0,16},{4,20},{8,24},{12,28},{16,0},{20,4},{24,8},{28,12},{1,17},{... | collective-permute-start | bytes 196616 | tf_op jit(solution)/shard_map/ppermute | solution.py:242
  6.4 6.4 %collective-permute-start.5 = (bf16[256,128]{1,0:T(8,128)(2,1)}, bf16[256,128]{1,0:T(8,128)(2,1)S(1)}, u32[]{:S(2)}, u32[]{:S(2)}) collective-permute-start(bf16[256,128]{1,0:T(8,128)(2,1)} %refs_1_.6), channel_id=1, source_target_pairs={{0,24},{4,28},{8,16},{12,20},{16,8},{20,12},{24,0},{28,4},{1,25},{... | collective-permute-start | bytes 196616 | tf_op jit(solution)/shard_map/ppermute | solution.py:242
  6.4 12.7 %collective-permute-start = (bf16[256,128]{1,0:T(8,128)(2,1)}, bf16[256,128]{1,0:T(8,128)(2,1)S(1)}, u32[]{:S(2)}, u32[]{:S(2)}) collective-permute-start(bf16[256,128]{1,0:T(8,128)(2,1)} %refs_1_.6), channel_id=1, source_target_pairs={{0,4},{4,0},{8,12},{12,8},{16,20},{20,16},{24,28},{28,24},{1,5},{5... | collective-permute-start | bytes 196616 | tf_op jit(solution)/shard_map/ppermute | solution.py:242
  8.1 11.0 %collective-permute-start.2 = (bf16[256,128]{1,0:T(8,128)(2,1)S(1)}, bf16[256,128]{1,0:T(8,128)(2,1)S(1)}, u32[]{:S(2)}, u32[]{:S(2)}) collective-permute-start(bf16[256,128]{1,0:T(8,128)(2,1)S(1)} %shard_map.113.refs_3_), channel_id=1, source_target_pairs={{0,4},{4,0},{8,12},{12,8},{16,20},{20,16},{24,28},{28,24},{1,5},{5... | collective-permute-start | bytes 196616 | tf_op jit(solution)/shard_map/ppermute | solution.py:242
  11.3 7.8 %collective-permute-start.4 = (bf16[256,128]{1,0:T(8,128)(2,1)S(1)}, bf16[256,128]{1,0:T(8,128)(2,1)S(1)}, u32[]{:S(2)}, u32[]{:S(2)}) collective-permute-start(bf16[256,128]{1,0:T(8,128)(2,1)S(1)} %collective-permute-done.3.refs_5_), channel_id=1, source_target_pairs={{0,4},{4,0},{8,12},{12,8},{16,20},{20,16},{24,28},{28,24},{1,5},{5... | collective-permute-start | bytes 196616 | tf_op jit(solution)/shard_map/ppermute | solution.py:242
  12.8 6.3 %collective-permute-start.6 = (bf16[256,128]{1,0:T(8,128)(2,1)S(1)}, bf16[256,128]{1,0:T(8,128)(2,1)S(1)}, u32[]{:S(2)}, u32[]{:S(2)}) collective-permute-start(bf16[256,128]{1,0:T(8,128)(2,1)S(1)} %collective-permute-done.5.refs_7_), channel_id=1, source_target_pairs={{0,4},{4,0},{8,12},{12,8},{16,20},{20,16},{24,28},{28,24},{1,5},{5... | collective-permute-start | bytes 196616 | tf_op jit(solution)/shard_map/ppermute | solution.py:242
  14.2 6.4 %collective-permute-start.8 = (bf16[256,256]{1,0:T(8,128)(2,1)S(1)}, bf16[256,256]{1,0:T(8,128)(2,1)S(1)}, u32[]{:S(2)}, u32[]{:S(2)}) collective-permute-start(bf16[256,256]{1,0:T(8,128)(2,1)S(1)} %copy-done.2), channel_id=1, source_target_pairs={{0,2},{1,3},{2,0},{3,1},{4,6},{5,7},{6,4},{7,5},{8,10},{9,11},{10,... | collective-permute-start | bytes 393224 | tf_op jit(solution)/shard_map/ppermute | solution.py:242
  16.5 2.6 %copy-start.1 = (bf16[256,128]{1,0:T(8,128)(2,1)S(1)}, bf16[256,128]{1,0:T(8,128)(2,1)}, u32[]{:S(2)}) copy-start(bf16[256,128]{1,0:T(8,128)(2,1)} %refs_1_.6) | copy-start | bytes 196612
  19.0 7.9 %copy-start.3 = (bf16[128,256]{1,0:T(8,128)(2,1)S(1)}, bf16[128,256]{1,0:T(8,128)(2,1)}, u32[]{:S(2)}) copy-start(bf16[128,256]{1,0:T(8,128)(2,1)} %refs_2_.1) | copy-start | bytes 196612
  19.0 7.9 %copy-start.4 = (f32[256]{0:T(256)S(1)}, f32[256]{0:T(256)}, u32[]{:S(2)}) copy-start(f32[256]{0:T(256)} %param.10) | copy-start | bytes 3076
  19.8 1.4 %collective-permute-start.7 = (bf16[512,128]{1,0:T(8,128)(2,1)S(1)}, bf16[512,128]{1,0:T(8,128)(2,1)S(1)}, u32[]{:S(2)}, u32[]{:S(2)}) collective-permute-start(bf16[512,128]{1,0:T(8,128)(2,1)S(1)} %shard_map.115), channel_id=1, source_target_pairs={{0,1},{1,0},{2,3},{3,2},{4,5},{5,4},{6,7},{7,6},{8,9},{9,8},{10,11... | collective-permute-start | bytes 393224 | tf_op jit(solution)/shard_map/ppermute | solution.py:242
  21.3 5.6 %collective-permute-start.9 = (bf16[512,128]{1,0:T(8,128)(2,1)S(1)}, bf16[512,128]{1,0:T(8,128)(2,1)S(1)}, u32[]{:S(2)}, u32[]{:S(2)}) collective-permute-start(bf16[512,128]{1,0:T(8,128)(2,1)S(1)} %shard_map.116.refs_0_), channel_id=1, source_target_pairs={{0,2},{1,3},{2,0},{3,1},{4,6},{5,7},{6,4},{7,5},{8,10},{9,11},{10,... | collective-permute-start | bytes 393224 | tf_op jit(solution)/shard_map/ppermute | solution.py:242
  27.3 1.4 %collective-permute-start.10 = (bf16[512,128]{1,0:T(8,128)(2,1)S(1)}, bf16[512,128]{1,0:T(8,128)(2,1)S(1)}, u32[]{:S(2)}, u32[]{:S(2)}) collective-permute-start(bf16[512,128]{1,0:T(8,128)(2,1)S(1)} %get-tuple-element.19.refs_1_), channel_id=1, source_target_pairs={{0,1},{1,0},{2,3},{3,2},{4,5},{5,4},{6,7},{7,6},{8,9},{9,8},{10,11... | collective-permute-start | bytes 393224 | tf_op jit(solution)/shard_map/ppermute | solution.py:242
  27.7 1.4 %collective-permute-start.11 = (bf16[80,256]{1,0:T(8,128)(2,1)S(1)}, bf16[80,256]{1,0:T(8,128)(2,1)S(1)}, u32[]{:S(2)}, u32[]{:S(2)}) collective-permute-start(bf16[80,256]{1,0:T(8,128)(2,1)S(1)} %get-tuple-element.26), channel_id=1, source_target_pairs={{0,1},{1,0},{2,3},{3,2},{4,5},{5,4},{6,7},{7,6},{8,9},{9,8},{10,11... | collective-permute-start | bytes 122888 | tf_op jit(solution)/shard_map/ppermute | solution.py:242
  29.1 4.1 %collective-permute-start.12 = (bf16[80,256]{1,0:T(8,128)(2,1)S(1)}, bf16[80,256]{1,0:T(8,128)(2,1)S(1)}, u32[]{:S(2)}, u32[]{:S(2)}) collective-permute-start(bf16[80,256]{1,0:T(8,128)(2,1)S(1)} %shard_map.121.refs_0_), channel_id=1, source_target_pairs={{0,8},{4,12},{8,0},{12,4},{16,24},{20,28},{24,16},{28,20},{1,9},{5... | collective-permute-start | bytes 122888 | tf_op jit(solution)/shard_map/ppermute | solution.py:242
  29.2 7.2 %collective-permute-start.16 = (bf16[2,128,256]{2,1,0:T(8,128)(2,1)S(1)}, bf16[2,128,256]{2,1,0:T(8,128)(2,1)S(1)}, u32[]{:S(2)}, u32[]{:S(2)}) collective-permute-start(bf16[2,128,256]{2,1,0:T(8,128)(2,1)S(1)} %shard_map.118.refs_4_.refs_2_), channel_id=1, source_target_pairs={{0,4},{4,0},{8,12},{12,8},{16,20},{20,16},{24,28},{28,24},{1,5},{5... | collective-permute-start | bytes 393224 | tf_op jit(solution)/shard_map/ppermute | solution.py:242
  33.6 6.0 %collective-permute-start.13 = (bf16[2,128,256]{2,1,0:T(8,128)(2,1)S(1)}, bf16[2,128,256]{2,1,0:T(8,128)(2,1)S(1)}, u32[]{:S(2)}, u32[]{:S(2)}) collective-permute-start(bf16[2,128,256]{2,1,0:T(8,128)(2,1)S(1)} %shard_map.123), channel_id=1, source_target_pairs={{0,8},{4,12},{8,0},{12,4},{16,24},{20,28},{24,16},{28,20},{1,9},{5... | collective-permute-start | bytes 393224 | tf_op jit(solution)/shard_map/ppermute | solution.py:242
  33.7 5.8 %collective-permute-start.14 = (bf16[80,256]{1,0:T(8,128)(2,1)S(1)}, bf16[80,256]{1,0:T(8,128)(2,1)S(1)}, u32[]{:S(2)}, u32[]{:S(2)}) collective-permute-start(bf16[80,256]{1,0:T(8,128)(2,1)S(1)} %shard_map.122.refs_3_.refs_0_), channel_id=1, source_target_pairs={{0,16},{4,20},{8,24},{12,28},{16,0},{20,4},{24,8},{28,12},{1,17},{... | collective-permute-start | bytes 122888 | tf_op jit(solution)/shard_map/ppermute | solution.py:242
  36.4 8.0 %collective-permute-start.17 = (bf16[128,256]{1,0:T(8,128)(2,1)S(1)}, bf16[128,256]{1,0:T(8,128)(2,1)S(1)}, u32[]{:S(2)}, u32[]{:S(2)}) collective-permute-start(bf16[128,256]{1,0:T(8,128)(2,1)S(1)} %get-tuple-element.27), channel_id=1, source_target_pairs={{0,16},{4,20},{8,24},{12,28},{16,0},{20,4},{24,8},{28,12},{1,17},{... | collective-permute-start | bytes 196616 | tf_op jit(solution)/shard_map/ppermute | solution.py:242
  37.5 6.9 %collective-permute-start.18 = (bf16[128,256]{1,0:T(8,128)(2,1)S(1)}, bf16[128,256]{1,0:T(8,128)(2,1)S(1)}, u32[]{:S(2)}, u32[]{:S(2)}) collective-permute-start(bf16[128,256]{1,0:T(8,128)(2,1)S(1)} %get-tuple-element.28), channel_id=1, source_target_pairs={{0,24},{4,28},{8,16},{12,20},{16,8},{20,12},{24,0},{28,4},{1,25},{... | collective-permute-start | bytes 196616 | tf_op jit(solution)/shard_map/ppermute | solution.py:242
  39.6 4.8 %collective-permute-start.15 = (bf16[208,256]{1,0:T(8,128)(2,1)S(1)}, bf16[208,256]{1,0:T(8,128)(2,1)S(1)}, u32[]{:S(2)}, u32[]{:S(2)}) collective-permute-start(bf16[208,256]{1,0:T(8,128)(2,1)S(1)} %shard_map.125), channel_id=1, source_target_pairs={{0,4},{4,0},{8,12},{12,8},{16,20},{20,16},{24,28},{28,24},{1,5},{5... | collective-permute-start | bytes 319496 | tf_op jit(solution)/shard_map/ppermute | solution.py:242
  44.5 1.3 %collective-permute-start.19 = (f32[64,256]{1,0:T(8,128)S(1)}, f32[64,256]{1,0:T(8,128)S(1)}, u32[]{:S(2)}, u32[]{:S(2)}) collective-permute-start(f32[64,256]{1,0:T(8,128)S(1)} %get-tuple-element.29.refs_1_), channel_id=1, source_target_pairs={{0,1},{1,0},{2,3},{3,2},{4,5},{5,4},{6,7},{7,6},{8,9},{9,8},{10,11... | collective-permute-start | bytes 196616 | tf_op jit(solution)/shard_map/ppermute | solution.py:242

commit v3 on v2

--- a/solution.py
+++ b/solution.py
@@ -11,6 +11,7 @@
 F32 = jnp.float32
 VMEM_LIMIT = 32 * 1024 * 1024
 IN_VMEM = pl.BlockSpec(memory_space=pltpu.VMEM)
+IN_SMEM = pl.BlockSpec(memory_space=pltpu.SMEM)
 IN_ANY = pl.BlockSpec(memory_space=pl.ANY)
 FIRST = 1 << 35
 SOON = 3 << 28
@@ -39,9 +40,11 @@
     target[...] = source[...]
 
 
-def lists_kernel(col_tiles, rows, cols, lists):
+def lists_kernel(col_tiles, rows, cols, count, lists):
     slots, wide = rows.shape[2], lists.shape[1]
-    by_slot = jnp.broadcast_to((rows[0] * col_tiles + cols[0]).astype(F32), (slots, slots))
+    live = lax.broadcasted_iota(jnp.int32, (1, slots), 1) < count[0, 0]
+    places = jnp.where(live, rows[0] * col_tiles + cols[0], wide)
+    by_slot = jnp.broadcast_to(places.astype(F32), (slots, slots))
     down = by_slot.T[:, :1]
     slot = lax.broadcasted_iota(jnp.int32, (slots, wide), 0)
     at = lax.broadcasted_iota(jnp.int32, (slots, wide), 1)
@@ -54,7 +57,7 @@
     lists[1:2, slots:] = jnp.full((1, wide - slots), slots, jnp.int32)
 
 
-def densify_kernel(lists, count, values, dense, head, after, many, sems):
+def densify_kernel(lists, values, dense, head, after, many, sems):
     slots, tile, _ = values.shape
     row_tiles, col_tiles = dense.shape[0] // tile, dense.shape[1] // tile
     moves = [
@@ -65,10 +68,9 @@
         copy.start()
     for copy in moves:
         copy.wait()
-    end = count[0, 0]
 
     def held(slot):
-        return jnp.where(slot < end, values[jnp.minimum(slot, slots - 1)], 0)
+        return jnp.where(slot < slots, values[jnp.minimum(slot, slots - 1)], 0)
 
     def write(row, found):
         top = pl.ds(pl.multiple_of(row * tile, tile), tile)
@@ -78,7 +80,7 @@
             two = after[0, one]
             dense[top, col * tile : (col + 1) * tile] = held(one) + held(two)
             many[found] = place
-            found += (after[0, two] < end).astype(jnp.int32)
+            found += (after[0, two] < slots).astype(jnp.int32)
         return found
 
     found = lax.fori_loop(0, row_tiles, write, jnp.int32(0))
@@ -97,7 +99,7 @@
         two = after[0, one]
         three = after[0, two]
         total = values[one].astype(F32) + values[two].astype(F32) + values[three].astype(F32)
-        _, total = lax.while_loop(lambda state: state[0] < end, more, (after[0, three], total))
+        _, total = lax.while_loop(lambda state: state[0] < slots, more, (after[0, three], total))
         dense[top, left] = total.astype(BF16)
         return carry
 
@@ -216,16 +218,16 @@
     near[rows:, :] = part[...]
 
 
-def gather_far_kernel(share_4, share_6, total):
-    total[...] = share_4[...].astype(F32) + share_6[...].astype(F32)
+def gather_far_kernel(kept, share_4, total):
+    total[...] = kept[2] + share_4[...].astype(F32)
 
 
 def gather_near_kernel(arrived, near, gathered, total):
     total[...] = arrived[0].astype(F32) + near[: total.shape[0], :].astype(F32) + gathered[...]
 
 
-def gather_own_kernel(kept, gathered, total):
-    total[...] = kept[2] + gathered[...]
+def gather_last_kernel(share_6, gathered, total):
+    total[...] = share_6[...].astype(F32) + gathered[...]
 
 
 def last_kernel(gathered, mine, theirs, bias, grad_features, grad_weight, grad_bias):
@@ -252,19 +254,20 @@
     whole = 2 * height * length * width_in
     shape = jax.ShapeDtypeStruct
 
-    far = [swap(features, "row", 4), swap(features, "row", 6)]
     near = call(relay_kernel, shape(features.shape, BF16), [IN_VMEM], flops=FIRST)(swap(features, "row", 2))
+    wide = 128 * pl.cdiv(max(positions, slots + 1), 128)
+    lists = call(
+        functools.partial(lists_kernel, length // tile), shape((2, wide), jnp.int32), [IN_VMEM, IN_VMEM, IN_SMEM], after=[near]
+    )(tile_rows, tile_cols, tile_count)
+    far_4, far_6 = swap(features, "row", 4), swap(features, "row", 6)
+    far_4 = call(relay_kernel, shape(features.shape, BF16), [IN_VMEM], after=[lists])(far_4)
     grad_out_x = swap(grad_out, "col", 2)
     y_1, y_near = swap(features, "row", 1), swap(near, "row", 1)
-    y_4, y_6 = swap(far[0], "row", 1), swap(far[1], "row", 1)
-    wide = 128 * pl.cdiv(max(positions, slots + 1), 128)
-    lists = call(
-        functools.partial(lists_kernel, length // tile), shape((2, wide), jnp.int32), [IN_VMEM] * 2
-    )(tile_rows, tile_cols)
+    y_4, y_6 = swap(far_4, "row", 1), swap(far_6, "row", 1)
     dense = call(
         densify_kernel,
         shape((height, length), BF16),
-        [IN_VMEM, pl.BlockSpec(memory_space=pltpu.SMEM), IN_VMEM],
+        [IN_VMEM] * 2,
         [
             pltpu.SMEM((1, wide), jnp.int32),
             pltpu.SMEM((1, wide), jnp.int32),
@@ -272,23 +275,25 @@
             pltpu.SemaphoreType.DMA((2,)),
         ],
         nbytes=2 * tile_values.size * 2,
-    )(lists, tile_count, tile_values.reshape(slots, tile, tile))
-    def forward(parts, dtype):
+        after=[y_near],
+    )(lists, tile_values.reshape(slots, tile, tile))
+
+    def forward(parts, dtype, after=()):
         return call(
             functools.partial(forward_kernel, parts),
             shape((2 * nodes, width_in), dtype),
             [IN_VMEM] * (1 + n_row),
             flops=whole // 2,
             nbytes=height * length,
-        )(dense, features, y_1, near, y_near, far[0], y_4, far[1], y_6)
-
-    core_share = swap(forward((1, 3), BF16), "col", 1)
+            after=after,
+        )(dense, features, y_1, near, y_near, far_4, y_4, far_6, y_6)
+
+    core_share = swap(forward((1, 3), BF16, [grad_out_x]), "col", 1)
     half = call(
         add_kernel,
         shape((2 * nodes, width_in), BF16),
         [IN_VMEM] * 2,
         nbytes=16 * nodes * width_in,
-        after=[grad_out_x],
     )(forward((0, 2), F32), core_share)
     half_x = swap(half, "col", 2)
     aggregate, grad_pre, hidden, grad_aggregate = call(
@@ -315,21 +320,6 @@
             after=after,
         )(dense, grad_aggregate, grad_aggregate_core)
 
-    sent_far = backward((5, 7), BF16)
-    arrived_far = swap(sent_far, "row", 1)
-    kept, hidden = call(
-        functools.partial(kept_kernel, (4, 6, 0, 1)),
-        [shape((4, width_in, nodes), F32), shape(hidden.shape, BF16)],
-        [IN_VMEM] * 4,
-        flops=whole // 2,
-        nbytes=height * length,
-        after=[sent_far],
-    )(dense, grad_aggregate, grad_aggregate_core, hidden)
-    turned = shape((width_in, nodes), BF16)
-    share_4, share_6 = call(far_kernel, [turned] * 2, [IN_VMEM] * 2, nbytes=16 * nodes * width_in)(
-        kept, arrived_far
-    )
-
     mine, theirs = call(
         weight_kernel,
         [shape((width_in // 2 + 16, width_out), BF16)] * 2,
@@ -338,6 +328,24 @@
         flops=4 * nodes * width_in * width_out,
         nbytes=8 * width_in * width_out,
     )(aggregate, grad_pre)
+    theirs = swap(theirs, "col", 1)
+
+    sent_far = backward((5, 7), BF16, [theirs])
+    arrived_far = swap(sent_far, "row", 1)
+    sent_near = backward((2, 3), BF16, [sent_far])
+    arrived_near = swap(sent_near, "row", 2)
+    kept, hidden = call(
+        functools.partial(kept_kernel, (4, 6, 0, 1)),
+        [shape((4, width_in, nodes), F32), shape(hidden.shape, BF16)],
+        [IN_VMEM] * 4,
+        flops=FIRST,
+        nbytes=height * length,
+        after=[sent_near],
+    )(dense, grad_aggregate, grad_aggregate_core, hidden)
+    turned = shape((width_in, nodes), BF16)
+    share_4, share_6 = call(far_kernel, [turned] * 2, [IN_VMEM] * 2, nbytes=16 * nodes * width_in)(
+        kept, arrived_far
+    )
 
     def merge(own, other, after=()):
         return call(
@@ -348,11 +356,9 @@
             after=after,
         )(own, other)
 
-    part = merge(mine, swap(theirs, "col", 1), [sent_far])
-    part = merge(part, swap(part, "row", 2), [kept])
-    sent_near = backward((2, 3), BF16, [part])
-    arrived_near = swap(sent_near, "row", 2)
-    part = merge(part, swap(part, "row", 4))
+    part = merge(mine, theirs, [sent_far])
+    part = merge(part, swap(part, "row", 4), [kept])
+    part = merge(part, swap(part, "row", 2))
     near = call(
         near_kernel,
         shape((width_in + part.shape[0], nodes), BF16),
@@ -367,11 +373,9 @@
         nbytes=8 * part.size,
     )(part, near)
     turned = shape((width_in, nodes), F32)
-    gathered = call(gather_far_kernel, turned, [IN_VMEM] * 2, flops=SOON)(
-        swap(share_4, "row", 4), swap(share_6, "row", 6)
-    )
+    gathered = call(gather_far_kernel, turned, [IN_VMEM] * 2, flops=SOON)(kept, swap(share_4, "row", 4))
     gathered = call(gather_near_kernel, turned, [IN_VMEM] * 3)(arrived_near, near, gathered)
-    gathered = call(gather_own_kernel, turned, [IN_VMEM] * 2, flops=FIRST)(kept, gathered)
+    gathered = call(gather_last_kernel, turned, [IN_VMEM] * 2, flops=FIRST)(swap(share_6, "row", 6), gathered)
     grad_features, grad_weight, grad_bias = call(
         last_kernel,
         [

time: 46.7 us -> 46.7 us (level)
  starting transfers between devices: 21.4 us -> 25.8 us
  waiting for transfers between devices: 16.1 us -> 11.8 us
    ppermute x20, starting transfers between devices: 21.4 us -> 25.8 us  [swap(): return lax.ppermute(value, axis, [(at, at ^ bits) for at in range(size)])]
    ppermute x20, waiting for transfers between devices: 16.1 us -> 11.8 us  [swap(): return lax.ppermute(value, axis, [(at, at ^ bits) for at in range(size)])]
    pallas_call x21 -> x22, Pallas kernels: 7.41 us -> 7.38 us  [call(): return lambda *args: run(*args, *after)]
  transfers between devices with their start and end apart: 20 -> 20, of which waited for: 7 -> 10; matrix products, arithmetic and copies ran while one was open for 0% -> 0% of each run, Pallas kernels for 13% -> 11%
where the time goes in v3:
time: 46.7 us; the launch traced here: 46.6 us
  starting transfers between devices  25.8 us (55%)
  waiting for transfers between devices  11.8 us (25%)
  Pallas kernels  7.38 us (16%)
  between operations  1.52 us (3%)
    ppermute x20, starting transfers between devices, swap(): return lax.ppermute(value, axis, [(at, at ^ bits) for at in range(size)])  25.8 us
    ppermute x20, waiting for transfers between devices, swap(): return lax.ppermute(value, axis, [(at, at ^ bits) for at in range(size)])  11.8 us
    pallas_call x22, Pallas kernels, call(): return lambda *args: run(*args, *after)  7.38 us
  transfers between devices with their start and end apart: 20, of which 10 were waited for; matrix products, arithmetic and copies ran while one was open for 0% of the time, Pallas kernels for 11%

profile of v3, /device:TPU:0, one launch (start us, length us, event | category | flops | bytes accessed | tf_op | source)
XLA Modules:
  0.0 46.6 jit_solution(4791160131416781513)
XLA Ops:
  0.6 3.1 %collective-permute-start = (bf16[256,128]{1,0:T(8,128)(2,1)}, bf16[256,128]{1,0:T(8,128)(2,1)S(1)}, u32[]{:S(2)}, u32[]{:S(2)}) collective-permute-start(bf16[256,128]{1,0:T(8,128)(2,1)} %refs_1_.5), channel_id=1, source_target_pairs={{0,8},{4,12},{8,0},{12,4},{16,24},{20,28},{24,16},{28,20},{1,9},{5... | collective-permute-start | bytes 196616 | tf_op jit(solution)/shard_map/ppermute | solution.py:244
  3.7 2.5 %collective-permute-start.5 = (bf16[256,128]{1,0:T(8,128)(2,1)}, bf16[256,128]{1,0:T(8,128)(2,1)S(1)}, u32[]{:S(2)}, u32[]{:S(2)}) collective-permute-start(bf16[256,128]{1,0:T(8,128)(2,1)} %refs_1_.5), channel_id=1, source_target_pairs={{0,24},{4,28},{8,16},{12,20},{16,8},{20,12},{24,0},{28,4},{1,25},{... | collective-permute-start | bytes 196616 | tf_op jit(solution)/shard_map/ppermute | solution.py:244
  6.2 0.1 collective-permute-start.3
  6.3 1.5 %collective-permute-start.2 = (bf16[256,128]{1,0:T(8,128)(2,1)}, bf16[256,128]{1,0:T(8,128)(2,1)S(1)}, u32[]{:S(2)}, u32[]{:S(2)}) collective-permute-start(bf16[256,128]{1,0:T(8,128)(2,1)} %refs_1_.5), channel_id=1, source_target_pairs={{0,4},{4,0},{8,12},{12,8},{16,20},{20,16},{24,28},{28,24},{1,5},{5... | collective-permute-start | bytes 196616 | tf_op jit(solution)/shard_map/ppermute | solution.py:244
  7.8 1.5 %collective-permute-start.7 = (bf16[256,256]{1,0:T(8,128)(2,1)}, bf16[256,256]{1,0:T(8,128)(2,1)S(1)}, u32[]{:S(2)}, u32[]{:S(2)}) collective-permute-start(bf16[256,256]{1,0:T(8,128)(2,1)} %refs_4_.1), channel_id=1, source_target_pairs={{0,2},{1,3},{2,0},{3,1},{4,6},{5,7},{6,4},{7,5},{8,10},{9,11},{10,... | collective-permute-start | bytes 393224 | tf_op jit(solution)/shard_map/ppermute | solution.py:244
  10.0 0.0 collective-permute-done.refs_0_
  10.0 0.6 %collective-permute-start.1 = (bf16[256,128]{1,0:T(8,128)(2,1)S(1)}, bf16[256,128]{1,0:T(8,128)(2,1)S(1)}, u32[]{:S(2)}, u32[]{:S(2)}) collective-permute-start(bf16[256,128]{1,0:T(8,128)(2,1)S(1)} %shard_map.111.refs_3_), channel_id=1, source_target_pairs={{0,4},{4,0},{8,12},{12,8},{16,20},{20,16},{24,28},{28,24},{1,5},{5... | collective-permute-start | bytes 196616 | tf_op jit(solution)/shard_map/ppermute | solution.py:244
  10.6 0.0 copy-done.5
  10.6 0.0 copy-done.6
  10.6 0.2 shard_map.112.refs_0_.refs_1_
  10.8 1.5 %collective-permute-start.6 = (bf16[256,128]{1,0:T(8,128)(2,1)S(1)}, bf16[256,128]{1,0:T(8,128)(2,1)S(1)}, u32[]{:S(2)}, u32[]{:S(2)}) collective-permute-start(bf16[256,128]{1,0:T(8,128)(2,1)S(1)} %collective-permute-done.5.refs_7_), channel_id=1, source_target_pairs={{0,4},{4,0},{8,12},{12,8},{16,20},{20,16},{24,28},{28,24},{1,5},{5... | collective-permute-start | bytes 196616 | tf_op jit(solution)/shard_map/ppermute | solution.py:244
  12.4 0.5 %collective-permute-done.3.refs_0_ = bf16[256,128]{1,0:T(8,128)(2,1)S(1)} collective-permute-done((bf16[256,128]{1,0:T(8,128)(2,1)}, bf16[256,128]{1,0:T(8,128)(2,1)S(1)}, u32[]{:S(2)}, u32[]{:S(2)}) %collective-permute-start.3) | collective-permute-done | bytes 65568 | tf_op jit(solution)/shard_map/ppermute | solution.py:244
  12.9 1.5 %collective-permute-start.4 = (bf16[256,128]{1,0:T(8,128)(2,1)S(1)}, bf16[256,128]{1,0:T(8,128)(2,1)S(1)}, u32[]{:S(2)}, u32[]{:S(2)}) collective-permute-start(bf16[256,128]{1,0:T(8,128)(2,1)S(1)} %shard_map.114.refs_5_), channel_id=1, source_target_pairs={{0,4},{4,0},{8,12},{12,8},{16,20},{20,16},{24,28},{28,24},{1,5},{5... | collective-permute-start | bytes 196616 | tf_op jit(solution)/shard_map/ppermute | solution.py:244
  14.4 0.0 collective-permute-done.1.refs_2_.refs_4_
  14.4 2.4 %shard_map.113.refs_0_ = bf16[1024,2048]{1,0:T(8,128)(2,1)S(1)} custom-call(s32[2,256]{1,0:T(2,128)S(1)} %shard_map.112.refs_0_.refs_1_, bf16[128,128,128]{2,1,0:T(8,128)(2,1)S(1)} %bitcast.3, bf16[256,128]{1,0:T(8,128)(2,1)S(1)} %collective-permute-done.1.refs_2_.refs_4_), custom_call_target="tpu_custom_call" | custom-call | bytes 8388608 | tf_op jit(solution)/shard_map/pallas_call | solution.py:36
  16.9 0.0 copy-start.2
  16.9 0.0 copy-start.3
  16.9 0.0 copy-start.4
  16.9 0.0 collective-permute-done.2.refs_2_
  16.9 0.2 collective-permute-done.4.refs_6_
  17.1 0.7 %shard_map.116 = bf16[512,128]{1,0:T(8,128)(2,1)S(1)} custom-call(bf16[1024,2048]{1,0:T(8,128)(2,1)S(1)} %shard_map.113.refs_0_, bf16[256,128]{1,0:T(8,128)(2,1)S(1)} %copy-done.1, bf16[256,128]{1,0:T(8,128)(2,1)S(1)} %collective-permute-done.2.refs_2_, bf16[256,128]{1,0:T(8,128)(2,1)S(1)} %shard_map.111.refs_3_, ...), custom_call_target="tpu_custom_call" | custom-call | flops 268435456 | bytes 2097152 | tf_op jit(solution)/shard_map/pallas_call | solution.py:36
  17.9 0.1 collective-permute-start.8
  17.9 0.7 %shard_map.115.refs_0_ = f32[512,128]{1,0:T(8,128)S(1)} custom-call(bf16[1024,2048]{1,0:T(8,128)(2,1)S(1)} %shard_map.113.refs_0_, bf16[256,128]{1,0:T(8,128)(2,1)S(1)} %copy-done.1, bf16[256,128]{1,0:T(8,128)(2,1)S(1)} %collective-permute-done.2.refs_2_, bf16[256,128]{1,0:T(8,128)(2,1)S(1)} %shard_map.111.refs_3_, ...), custom_call_target="tpu_custom_call" | custom-call | flops 268435456 | bytes 2097152 | tf_op jit(solution)/shard_map/pallas_call | solution.py:36
  18.7 0.6 %collective-permute-done.8.refs_1_ = bf16[512,128]{1,0:T(8,128)(2,1)S(1)} collective-permute-done((bf16[512,128]{1,0:T(8,128)(2,1)S(1)}, bf16[512,128]{1,0:T(8,128)(2,1)S(1)}, u32[]{:S(2)}, u32[]{:S(2)}) %collective-permute-start.8) | collective-permute-done | bytes 131104 | tf_op jit(solution)/shard_map/ppermute | solution.py:244
  19.3 1.6 %collective-permute-start.9 = (bf16[512,128]{1,0:T(8,128)(2,1)S(1)}, bf16[512,128]{1,0:T(8,128)(2,1)S(1)}, u32[]{:S(2)}, u32[]{:S(2)}) collective-permute-start(bf16[512,128]{1,0:T(8,128)(2,1)S(1)} %shard_map.117.refs_0_), channel_id=1, source_target_pairs={{0,2},{1,3},{2,0},{3,1},{4,6},{5,7},{6,4},{7,5},{8,10},{9,11},{10,... | collective-permute-start | bytes 393224 | tf_op jit(solution)/shard_map/ppermute | solution.py:244
  20.9 4.1 %collective-permute-done.9.refs_1_ = bf16[512,128]{1,0:T(8,128)(2,1)S(1)} collective-permute-done((bf16[512,128]{1,0:T(8,128)(2,1)S(1)}, bf16[512,128]{1,0:T(8,128)(2,1)S(1)}, u32[]{:S(2)}, u32[]{:S(2)}) %collective-permute-start.9) | collective-permute-done | bytes 131104 | tf_op jit(solution)/shard_map/ppermute | solution.py:244
  24.9 0.4 shard_map.118
  25.4 0.1 collective-permute-start.10
  25.5 0.3 shard_map.119
  25.7 0.6 %collective-permute-start.11 = (bf16[80,256]{1,0:T(8,128)(2,1)S(1)}, bf16[80,256]{1,0:T(8,128)(2,1)S(1)}, u32[]{:S(2)}, u32[]{:S(2)}) collective-permute-start(bf16[80,256]{1,0:T(8,128)(2,1)S(1)} %get-tuple-element.23), channel_id=1, source_target_pairs={{0,1},{1,0},{2,3},{3,2},{4,5},{5,4},{6,7},{7,6},{8,9},{9,8},{10,11... | collective-permute-start | bytes 122888 | tf_op jit(solution)/shard_map/ppermute | solution.py:244
  26.3 0.9 %collective-permute-done.11.refs_3_.refs_1_ = bf16[80,256]{1,0:T(8,128)(2,1)S(1)} collective-permute-done((bf16[80,256]{1,0:T(8,128)(2,1)S(1)}, bf16[80,256]{1,0:T(8,128)(2,1)S(1)}, u32[]{:S(2)}, u32[]{:S(2)}) %collective-permute-start.11) | collective-permute-done | bytes 40992 | tf_op jit(solution)/shard_map/ppermute | solution.py:244
  27.2 0.3 shard_map.120.refs_3_.refs_2_
  27.5 1.6 %collective-permute-start.12 = (bf16[2,128,256]{2,1,0:T(8,128)(2,1)S(1)}, bf16[2,128,256]{2,1,0:T(8,128)(2,1)S(1)}, u32[]{:S(2)}, u32[]{:S(2)}) collective-permute-start(bf16[2,128,256]{2,1,0:T(8,128)(2,1)S(1)} %shard_map.120.refs_3_.refs_2_), channel_id=1, source_target_pairs={{0,4},{4,0},{8,12},{12,8},{16,20},{20,16},{24,28},{28,24},{1,5},{5... | collective-permute-start | bytes 393224 | tf_op jit(solution)/shard_map/ppermute | solution.py:244
  29.1 2.1 %collective-permute-start.15 = (bf16[80,256]{1,0:T(8,128)(2,1)S(1)}, bf16[80,256]{1,0:T(8,128)(2,1)S(1)}, u32[]{:S(2)}, u32[]{:S(2)}) collective-permute-start(bf16[80,256]{1,0:T(8,128)(2,1)S(1)} %shard_map.124.refs_0_), channel_id=1, source_target_pairs={{0,16},{4,20},{8,24},{12,28},{16,0},{20,4},{24,8},{28,12},{1,17},{... | collective-permute-start | bytes 122888 | tf_op jit(solution)/shard_map/ppermute | solution.py:244
  31.2 0.3 shard_map.121.refs_4_
  31.5 1.0 %collective-permute-start.14 = (bf16[2,128,256]{2,1,0:T(8,128)(2,1)S(1)}, bf16[2,128,256]{2,1,0:T(8,128)(2,1)S(1)}, u32[]{:S(2)}, u32[]{:S(2)}) collective-permute-start(bf16[2,128,256]{2,1,0:T(8,128)(2,1)S(1)} %shard_map.121.refs_4_), channel_id=1, source_target_pairs={{0,8},{4,12},{8,0},{12,4},{16,24},{20,28},{24,16},{28,20},{1,9},{5... | collective-permute-start | bytes 393224 | tf_op jit(solution)/shard_map/ppermute | solution.py:244
  32.5 1.0 %shard_map.122 = (f32[4,128,256]{2,1,0:T(8,128)S(1)}, bf16[256,256]{1,0:T(8,128)(2,1)}) custom-call(bf16[1024,2048]{1,0:T(8,128)(2,1)S(1)} %shard_map.113.refs_0_, bf16[512,128]{1,0:T(8,128)(2,1)S(1)} %get-tuple-element.19.refs_1_, bf16[512,128]{1,0:T(8,128)(2,1)S(1)} %collective-permute-done.10.refs_2_, bf16[256,256]{1,0:T(8,128)(2,1)S(1)} %get-tuple-element.20.refs_3_, ...), custom_call_target="tpu_custom_call" | custom-call | flops 34359738368 | bytes 2097152 | tf_op jit(solution)/shard_map/pallas_call | solution.py:36
  33.5 1.0 %collective-permute-done.15.refs_1_ = bf16[80,256]{1,0:T(8,128)(2,1)S(1)} collective-permute-done((bf16[80,256]{1,0:T(8,128)(2,1)S(1)}, bf16[80,256]{1,0:T(8,128)(2,1)S(1)}, u32[]{:S(2)}, u32[]{:S(2)}) %collective-permute-start.15) | collective-permute-done | bytes 40992 | tf_op jit(solution)/shard_map/ppermute | solution.py:244
  34.6 1.4 %collective-permute-start.16 = (bf16[80,256]{1,0:T(8,128)(2,1)S(1)}, bf16[80,256]{1,0:T(8,128)(2,1)S(1)}, u32[]{:S(2)}, u32[]{:S(2)}) collective-permute-start(bf16[80,256]{1,0:T(8,128)(2,1)S(1)} %shard_map.125.refs_0_), channel_id=1, source_target_pairs={{0,8},{4,12},{8,0},{12,4},{16,24},{20,28},{24,16},{28,20},{1,9},{5... | collective-permute-start | bytes 122888 | tf_op jit(solution)/shard_map/ppermute | solution.py:244
  36.1 1.3 %collective-permute-start.18 = (bf16[128,256]{1,0:T(8,128)(2,1)S(1)}, bf16[128,256]{1,0:T(8,128)(2,1)S(1)}, u32[]{:S(2)}, u32[]{:S(2)}) collective-permute-start(bf16[128,256]{1,0:T(8,128)(2,1)S(1)} %get-tuple-element.28), channel_id=1, source_target_pairs={{0,16},{4,20},{8,24},{12,28},{16,0},{20,4},{24,8},{28,12},{1,17},{... | collective-permute-start | bytes 196616 | tf_op jit(solution)/shard_map/ppermute | solution.py:244
  37.4 1.3 %collective-permute-done.16.refs_1_ = bf16[80,256]{1,0:T(8,128)(2,1)S(1)} collective-permute-done((bf16[80,256]{1,0:T(8,128)(2,1)S(1)}, bf16[80,256]{1,0:T(8,128)(2,1)S(1)}, u32[]{:S(2)}, u32[]{:S(2)}) %collective-permute-start.16) | collective-permute-done | bytes 40992 | tf_op jit(solution)/shard_map/ppermute | solution.py:244
  38.7 1.0 %collective-permute-start.17 = (bf16[208,256]{1,0:T(8,128)(2,1)S(1)}, bf16[208,256]{1,0:T(8,128)(2,1)S(1)}, u32[]{:S(2)}, u32[]{:S(2)}) collective-permute-start(bf16[208,256]{1,0:T(8,128)(2,1)S(1)} %shard_map.127), channel_id=1, source_target_pairs={{0,4},{4,0},{8,12},{12,8},{16,20},{20,16},{24,28},{28,24},{1,5},{5... | collective-permute-start | bytes 319496 | tf_op jit(solution)/shard_map/ppermute | solution.py:244
  39.8 2.7 %collective-permute-start.13 = (bf16[128,256]{1,0:T(8,128)(2,1)S(1)}, bf16[128,256]{1,0:T(8,128)(2,1)S(1)}, u32[]{:S(2)}, u32[]{:S(2)}) collective-permute-start(bf16[128,256]{1,0:T(8,128)(2,1)S(1)} %get-tuple-element.26), channel_id=1, source_target_pairs={{0,24},{4,28},{8,16},{12,20},{16,8},{20,12},{24,0},{28,4},{1,25},{... | collective-permute-start | bytes 196616 | tf_op jit(solution)/shard_map/ppermute | solution.py:244
  42.5 0.7 %collective-permute-done.18.refs_1_ = bf16[128,256]{1,0:T(8,128)(2,1)S(1)} collective-permute-done((bf16[128,256]{1,0:T(8,128)(2,1)S(1)}, bf16[128,256]{1,0:T(8,128)(2,1)S(1)}, u32[]{:S(2)}, u32[]{:S(2)}) %collective-permute-start.18) | collective-permute-done | bytes 65568 | tf_op jit(solution)/shard_map/ppermute | solution.py:244
  43.2 0.3 collective-permute-done.17.refs_1_
  43.5 0.1 collective-permute-start.19
  43.6 2.2 %collective-permute-done.13.refs_0_ = bf16[128,256]{1,0:T(8,128)(2,1)S(1)} collective-permute-done((bf16[128,256]{1,0:T(8,128)(2,1)S(1)}, bf16[128,256]{1,0:T(8,128)(2,1)S(1)}, u32[]{:S(2)}, u32[]{:S(2)}) %collective-permute-start.13) | collective-permute-done | bytes 65568 | tf_op jit(solution)/shard_map/ppermute | solution.py:244
  45.8 0.7 %shard_map.132 = (bf16[256,128]{1,0:T(8,128)(2,1)}, f32[128,256]{1,0:T(8,128)}, f32[1,256]{1,0:T(1,128)}) custom-call(f32[128,256]{1,0:T(8,128)S(1)} %shard_map.130.refs_0_, f32[64,256]{1,0:T(8,128)S(1)} %get-tuple-element.29.refs_1_, f32[64,256]{1,0:T(8,128)S(1)} %collective-permute-done.19.refs_2_, f32[1,256]{1,0:T(1,128)S(1)} %get-tuple-element.30.refs_3_), custom_call_target="tpu_custom_call" | custom-call | bytes 524288 | tf_op jit(solution)/shard_map/pallas_call | solution.py:36
  (28 shorter events, 0.3 us)
Async XLA Ops:
  0.6 9.4 %collective-permute-start = (bf16[256,128]{1,0:T(8,128)(2,1)}, bf16[256,128]{1,0:T(8,128)(2,1)S(1)}, u32[]{:S(2)}, u32[]{:S(2)}) collective-permute-start(bf16[256,128]{1,0:T(8,128)(2,1)} %refs_1_.5), channel_id=1, source_target_pairs={{0,8},{4,12},{8,0},{12,4},{16,24},{20,28},{24,16},{28,20},{1,9},{5... | collective-permute-start | bytes 196616 | tf_op jit(solution)/shard_map/ppermute | solution.py:244
  3.7 7.1 %collective-permute-start.5 = (bf16[256,128]{1,0:T(8,128)(2,1)}, bf16[256,128]{1,0:T(8,128)(2,1)S(1)}, u32[]{:S(2)}, u32[]{:S(2)}) collective-permute-start(bf16[256,128]{1,0:T(8,128)(2,1)} %refs_1_.5), channel_id=1, source_target_pairs={{0,24},{4,28},{8,16},{12,20},{16,8},{20,12},{24,0},{28,4},{1,25},{... | collective-permute-start | bytes 196616 | tf_op jit(solution)/shard_map/ppermute | solution.py:244
  6.2 6.7 %collective-permute-start.3 = (bf16[256,128]{1,0:T(8,128)(2,1)}, bf16[256,128]{1,0:T(8,128)(2,1)S(1)}, u32[]{:S(2)}, u32[]{:S(2)}) collective-permute-start(bf16[256,128]{1,0:T(8,128)(2,1)} %refs_1_.5), channel_id=1, source_target_pairs={{0,16},{4,20},{8,24},{12,28},{16,0},{20,4},{24,8},{28,12},{1,17},{... | collective-permute-start | bytes 196616 | tf_op jit(solution)/shard_map/ppermute | solution.py:244
  6.3 10.6 %collective-permute-start.2 = (bf16[256,128]{1,0:T(8,128)(2,1)}, bf16[256,128]{1,0:T(8,128)(2,1)S(1)}, u32[]{:S(2)}, u32[]{:S(2)}) collective-permute-start(bf16[256,128]{1,0:T(8,128)(2,1)} %refs_1_.5), channel_id=1, source_target_pairs={{0,4},{4,0},{8,12},{12,8},{16,20},{20,16},{24,28},{28,24},{1,5},{5... | collective-permute-start | bytes 196616 | tf_op jit(solution)/shard_map/ppermute | solution.py:244
  7.8 9.3 %collective-permute-start.7 = (bf16[256,256]{1,0:T(8,128)(2,1)}, bf16[256,256]{1,0:T(8,128)(2,1)S(1)}, u32[]{:S(2)}, u32[]{:S(2)}) collective-permute-start(bf16[256,256]{1,0:T(8,128)(2,1)} %refs_4_.1), channel_id=1, source_target_pairs={{0,2},{1,3},{2,0},{3,1},{4,6},{5,7},{6,4},{7,5},{8,10},{9,11},{10,... | collective-permute-start | bytes 393224 | tf_op jit(solution)/shard_map/ppermute | solution.py:244
  10.0 0.7 %copy-start.5 = (s32[1,1,128]{2,1,0:T(1,128)S(1)}, s32[1,1,128]{2,1,0:T(1,128)}, u32[]{:S(2)}) copy-start(s32[1,1,128]{2,1,0:T(1,128)} %refs_0_.1) | copy-start | bytes 1540
  10.0 0.7 %copy-start.6 = (s32[1,1,128]{2,1,0:T(1,128)S(1)}, s32[1,1,128]{2,1,0:T(1,128)}, u32[]{:S(2)}) copy-start(s32[1,1,128]{2,1,0:T(1,128)} %refs_1_.3) | copy-start | bytes 1540
  10.0 4.4 %copy-start = (bf16[1,1,128,128,128]{4,3,2,1,0:T(8,128)(2,1)S(1)}, bf16[1,1,128,128,128]{4,3,2,1,0:T(8,128)(2,1)}, u32[]{:S(2)}) copy-start(bf16[1,1,128,128,128]{4,3,2,1,0:T(8,128)(2,1)} %param.12) | copy-start | bytes 12582916
  10.0 4.4 %collective-permute-start.1 = (bf16[256,128]{1,0:T(8,128)(2,1)S(1)}, bf16[256,128]{1,0:T(8,128)(2,1)S(1)}, u32[]{:S(2)}, u32[]{:S(2)}) collective-permute-start(bf16[256,128]{1,0:T(8,128)(2,1)S(1)} %shard_map.111.refs_3_), channel_id=1, source_target_pairs={{0,4},{4,0},{8,12},{12,8},{16,20},{20,16},{24,28},{28,24},{1,5},{5... | collective-permute-start | bytes 196616 | tf_op jit(solution)/shard_map/ppermute | solution.py:244
  10.8 6.1 %collective-permute-start.6 = (bf16[256,128]{1,0:T(8,128)(2,1)S(1)}, bf16[256,128]{1,0:T(8,128)(2,1)S(1)}, u32[]{:S(2)}, u32[]{:S(2)}) collective-permute-start(bf16[256,128]{1,0:T(8,128)(2,1)S(1)} %collective-permute-done.5.refs_7_), channel_id=1, source_target_pairs={{0,4},{4,0},{8,12},{12,8},{16,20},{20,16},{24,28},{28,24},{1,5},{5... | collective-permute-start | bytes 196616 | tf_op jit(solution)/shard_map/ppermute | solution.py:244
  12.9 4.3 %collective-permute-start.4 = (bf16[256,128]{1,0:T(8,128)(2,1)S(1)}, bf16[256,128]{1,0:T(8,128)(2,1)S(1)}, u32[]{:S(2)}, u32[]{:S(2)}) collective-permute-start(bf16[256,128]{1,0:T(8,128)(2,1)S(1)} %shard_map.114.refs_5_), channel_id=1, source_target_pairs={{0,4},{4,0},{8,12},{12,8},{16,20},{20,16},{24,28},{28,24},{1,5},{5... | collective-permute-start | bytes 196616 | tf_op jit(solution)/shard_map/ppermute | solution.py:244
  14.4 2.7 %copy-start.1 = (bf16[256,128]{1,0:T(8,128)(2,1)S(1)}, bf16[256,128]{1,0:T(8,128)(2,1)}, u32[]{:S(2)}) copy-start(bf16[256,128]{1,0:T(8,128)(2,1)} %refs_1_.5) | copy-start | bytes 196612
  16.9 8.1 %copy-start.2 = (bf16[256,256]{1,0:T(8,128)(2,1)S(1)}, bf16[256,256]{1,0:T(8,128)(2,1)}, u32[]{:S(2)}) copy-start(bf16[256,256]{1,0:T(8,128)(2,1)} %refs_4_.1) | copy-start | bytes 393220
  16.9 8.1 %copy-start.3 = (bf16[128,256]{1,0:T(8,128)(2,1)S(1)}, bf16[128,256]{1,0:T(8,128)(2,1)}, u32[]{:S(2)}) copy-start(bf16[128,256]{1,0:T(8,128)(2,1)} %refs_2_.2) | copy-start | bytes 196612
  16.9 8.1 %copy-start.4 = (f32[256]{0:T(256)S(1)}, f32[256]{0:T(256)}, u32[]{:S(2)}) copy-start(f32[256]{0:T(256)} %param.10) | copy-start | bytes 3076
  17.9 1.4 %collective-permute-start.8 = (bf16[512,128]{1,0:T(8,128)(2,1)S(1)}, bf16[512,128]{1,0:T(8,128)(2,1)S(1)}, u32[]{:S(2)}, u32[]{:S(2)}) collective-permute-start(bf16[512,128]{1,0:T(8,128)(2,1)S(1)} %shard_map.116), channel_id=1, source_target_pairs={{0,1},{1,0},{2,3},{3,2},{4,5},{5,4},{6,7},{7,6},{8,9},{9,8},{10,11... | collective-permute-start | bytes 393224 | tf_op jit(solution)/shard_map/ppermute | solution.py:244
  19.3 5.6 %collective-permute-start.9 = (bf16[512,128]{1,0:T(8,128)(2,1)S(1)}, bf16[512,128]{1,0:T(8,128)(2,1)S(1)}, u32[]{:S(2)}, u32[]{:S(2)}) collective-permute-start(bf16[512,128]{1,0:T(8,128)(2,1)S(1)} %shard_map.117.refs_0_), channel_id=1, source_target_pairs={{0,2},{1,3},{2,0},{3,1},{4,6},{5,7},{6,4},{7,5},{8,10},{9,11},{10,... | collective-permute-start | bytes 393224 | tf_op jit(solution)/shard_map/ppermute | solution.py:244
  25.4 1.8 %collective-permute-start.10 = (bf16[512,128]{1,0:T(8,128)(2,1)S(1)}, bf16[512,128]{1,0:T(8,128)(2,1)S(1)}, u32[]{:S(2)}, u32[]{:S(2)}) collective-permute-start(bf16[512,128]{1,0:T(8,128)(2,1)S(1)} %get-tuple-element.19.refs_1_), channel_id=1, source_target_pairs={{0,1},{1,0},{2,3},{3,2},{4,5},{5,4},{6,7},{7,6},{8,9},{9,8},{10,11... | collective-permute-start | bytes 393224 | tf_op jit(solution)/shard_map/ppermute | solution.py:244
  25.7 1.4 %collective-permute-start.11 = (bf16[80,256]{1,0:T(8,128)(2,1)S(1)}, bf16[80,256]{1,0:T(8,128)(2,1)S(1)}, u32[]{:S(2)}, u32[]{:S(2)}) collective-permute-start(bf16[80,256]{1,0:T(8,128)(2,1)S(1)} %get-tuple-element.23), channel_id=1, source_target_pairs={{0,1},{1,0},{2,3},{3,2},{4,5},{5,4},{6,7},{7,6},{8,9},{9,8},{10,11... | collective-permute-start | bytes 122888 | tf_op jit(solution)/shard_map/ppermute | solution.py:244
  27.5 8.5 %collective-permute-start.12 = (bf16[2,128,256]{2,1,0:T(8,128)(2,1)S(1)}, bf16[2,128,256]{2,1,0:T(8,128)(2,1)S(1)}, u32[]{:S(2)}, u32[]{:S(2)}) collective-permute-start(bf16[2,128,256]{2,1,0:T(8,128)(2,1)S(1)} %shard_map.120.refs_3_.refs_2_), channel_id=1, source_target_pairs={{0,4},{4,0},{8,12},{12,8},{16,20},{20,16},{24,28},{28,24},{1,5},{5... | collective-permute-start | bytes 393224 | tf_op jit(solution)/shard_map/ppermute | solution.py:244
  29.1 5.5 %collective-permute-start.15 = (bf16[80,256]{1,0:T(8,128)(2,1)S(1)}, bf16[80,256]{1,0:T(8,128)(2,1)S(1)}, u32[]{:S(2)}, u32[]{:S(2)}) collective-permute-start(bf16[80,256]{1,0:T(8,128)(2,1)S(1)} %shard_map.124.refs_0_), channel_id=1, source_target_pairs={{0,16},{4,20},{8,24},{12,28},{16,0},{20,4},{24,8},{28,12},{1,17},{... | collective-permute-start | bytes 122888 | tf_op jit(solution)/shard_map/ppermute | solution.py:244
  31.5 7.2 %collective-permute-start.14 = (bf16[2,128,256]{2,1,0:T(8,128)(2,1)S(1)}, bf16[2,128,256]{2,1,0:T(8,128)(2,1)S(1)}, u32[]{:S(2)}, u32[]{:S(2)}) collective-permute-start(bf16[2,128,256]{2,1,0:T(8,128)(2,1)S(1)} %shard_map.121.refs_4_), channel_id=1, source_target_pairs={{0,8},{4,12},{8,0},{12,4},{16,24},{20,28},{24,16},{28,20},{1,9},{5... | collective-permute-start | bytes 393224 | tf_op jit(solution)/shard_map/ppermute | solution.py:244
  34.6 4.1 %collective-permute-start.16 = (bf16[80,256]{1,0:T(8,128)(2,1)S(1)}, bf16[80,256]{1,0:T(8,128)(2,1)S(1)}, u32[]{:S(2)}, u32[]{:S(2)}) collective-permute-start(bf16[80,256]{1,0:T(8,128)(2,1)S(1)} %shard_map.125.refs_0_), channel_id=1, source_target_pairs={{0,8},{4,12},{8,0},{12,4},{16,24},{20,28},{24,16},{28,20},{1,9},{5... | collective-permute-start | bytes 122888 | tf_op jit(solution)/shard_map/ppermute | solution.py:244
  36.1 7.1 %collective-permute-start.18 = (bf16[128,256]{1,0:T(8,128)(2,1)S(1)}, bf16[128,256]{1,0:T(8,128)(2,1)S(1)}, u32[]{:S(2)}, u32[]{:S(2)}) collective-permute-start(bf16[128,256]{1,0:T(8,128)(2,1)S(1)} %get-tuple-element.28), channel_id=1, source_target_pairs={{0,16},{4,20},{8,24},{12,28},{16,0},{20,4},{24,8},{28,12},{1,17},{... | collective-permute-start | bytes 196616 | tf_op jit(solution)/shard_map/ppermute | solution.py:244
  38.7 4.8 %collective-permute-start.17 = (bf16[208,256]{1,0:T(8,128)(2,1)S(1)}, bf16[208,256]{1,0:T(8,128)(2,1)S(1)}, u32[]{:S(2)}, u32[]{:S(2)}) collective-permute-start(bf16[208,256]{1,0:T(8,128)(2,1)S(1)} %shard_map.127), channel_id=1, source_target_pairs={{0,4},{4,0},{8,12},{12,8},{16,20},{20,16},{24,28},{28,24},{1,5},{5... | collective-permute-start | bytes 319496 | tf_op jit(solution)/shard_map/ppermute | solution.py:244
  39.8 6.1 %collective-permute-start.13 = (bf16[128,256]{1,0:T(8,128)(2,1)S(1)}, bf16[128,256]{1,0:T(8,128)(2,1)S(1)}, u32[]{:S(2)}, u32[]{:S(2)}) collective-permute-start(bf16[128,256]{1,0:T(8,128)(2,1)S(1)} %get-tuple-element.26), channel_id=1, source_target_pairs={{0,24},{4,28},{8,16},{12,20},{16,8},{20,12},{24,0},{28,4},{1,25},{... | collective-permute-start | bytes 196616 | tf_op jit(solution)/shard_map/ppermute | solution.py:244
  43.5 2.3 %collective-permute-start.19 = (f32[64,256]{1,0:T(8,128)S(1)}, f32[64,256]{1,0:T(8,128)S(1)}, u32[]{:S(2)}, u32[]{:S(2)}) collective-permute-start(f32[64,256]{1,0:T(8,128)S(1)} %get-tuple-element.29.refs_1_), channel_id=1, source_target_pairs={{0,1},{1,0},{2,3},{3,2},{4,5},{5,4},{6,7},{7,6},{8,9},{9,8},{10,11... | collective-permute-start | bytes 196616 | tf_op jit(solution)/shard_map/ppermute | solution.py:244
